TPU v7x, 256 devices: a whole 4x4x8 slice. The times are simulated.
256 devices in a mesh: tm: 4 (over x), row: 8 (over z), col: 8 (over y, core).
Axes of the slice: x: 4, y: 4, z: 8, core: 2. Of those that a mesh axis runs over, the one named last changes fastest.
Arguments:
- latents: bfloat16 [8, 128, 128, 256], P('tm', 'row', 'col'), may hold values from -33 to 33
- gain_one: float32 [256], replicated, may hold values from 0.1 to 1.9
- shift_one: float32 [256], replicated, may hold values from -3 to 3
- kernel_one: bfloat16 [3, 3, 3, 256, 256], replicated, may hold values from -0.078125 to 0.078125
- offset_one: float32 [256], replicated, may hold values from -3 to 3
- gain_two: float32 [256], replicated, may hold values from 0.1 to 1.9
- shift_two: float32 [256], replicated, may hold values from -3 to 3
- kernel_two: bfloat16 [3, 3, 3, 256, 256], replicated, may hold values from -0.078125 to 0.078125
- offset_two: float32 [256], replicated, may hold values from -3 to 3
- kernel_three: bfloat16 [3, 3, 3, 256, 256], replicated, may hold values from -0.078125 to 0.078125
- offset_three: float32 [256], replicated, may hold values from -3 to 3
Outputs:
- decoded: bfloat16 [8, 256, 256, 256], P('tm', 'row', 'col')
All inputs are finite; a program needn't handle non-finite values.
Results may differ from a plain program's by a relative error of at most 0.006.
Values may be sent and summed in bfloat16 or wider, within the bound.
No kernel may reach another device: no remote copies, remote signals or barrier semaphores. Data moves between devices by JAX's collectives and lax.ppermute only.
A program may use at most 128 MiB of HBM per device.

v0:
```python
import jax
import jax.numpy as jnp
from jax import lax
from jax.experimental import pallas as pl
from jax.experimental.layout import Layout, with_layout_constraint
from jax.experimental.pallas import tpu as pltpu
from jax.sharding import PartitionSpec as P

GROUPS = 32
EPSILON = 1e-06
AXES = ("tm", "row", "col")
F32 = jnp.float32
BF16 = jnp.bfloat16
VMEM = pl.BlockSpec(memory_space=pltpu.VMEM)
ANY = pl.BlockSpec(memory_space=pl.ANY)
WIDE = 22
PITCH = 20


def exact_dot(a, b):
    return jnp.dot(a, b, precision=lax.Precision.HIGHEST, preferred_element_type=F32)


def iotas(shape):
    return lax.broadcasted_iota(jnp.int32, shape, 0), lax.broadcasted_iota(jnp.int32, shape, 1)


def lane_to_channel(first, channels):
    lane, channel = iotas((128, channels))
    return (lane % 64 == channel // (channels // GROUPS) + first).astype(F32)


def channel_to_lane(channels):
    channel, lane = iotas((channels, 128))
    return (lane % GROUPS == channel // (channels // GROUPS)).astype(F32)


def eight(row):
    return jnp.broadcast_to(row, (8, row.shape[1]))


def own_stats(flat):
    rows, channels = flat.shape
    to_lane = channel_to_lane(channels)
    count = rows * (channels // GROUPS)
    mean = exact_dot(eight(jnp.sum(flat, axis=0, keepdims=True)), to_lane) / count
    own_mean = exact_dot(jnp.where(iotas(mean.shape)[1] < 64, mean, 0.0), lane_to_channel(0, channels))
    centered = flat - own_mean[:1]
    spread = exact_dot(eight(jnp.sum(centered * centered, axis=0, keepdims=True)), to_lane)
    return jnp.where(iotas(mean.shape)[1] % 64 < GROUPS, mean, spread)


def norm_terms(every, gain, cells):
    channels = gain.shape[1]
    devices = 2 * every.shape[0]
    count = cells * (channels // GROUPS)
    total = eight(jnp.sum(every, axis=0, keepdims=True))
    source, lane = iotas((128, 128))
    spread_mean = ((source % 64 < GROUPS) & (source % GROUPS == lane % GROUPS)).astype(F32)
    off = every - exact_dot(total, spread_mean)[:1] / devices
    between = eight(jnp.sum(off * off, axis=0, keepdims=True))
    to_mean = lane_to_channel(0, channels)
    spread = exact_dot(total, lane_to_channel(GROUPS, channels)) + exact_dot(between, to_mean) * count
    var = spread / (count * devices)
    mean = exact_dot(total, to_mean) / devices
    return mean[:1], gain * lax.rsqrt(var[:1] + EPSILON)


def norm_silu(value, mean, factor, shift):
    normed = (value.astype(F32) - mean) * factor + shift
    half = 0.5 * normed
    return half * jnp.tanh(half) + half


def place():
    at = [lax.axis_index(axis) for axis in AXES]
    return (
        at[0],
        at[1] == 0,
        at[1] == lax.axis_size("row") - 1,
        at[2] == 0,
        at[2] == lax.axis_size("col") - 1,
    )


def fetch_taps(kernel_ref, held_ref, sems, rows):
    copies = []
    for p in rows:
        for q in range(3):
            copy = pltpu.make_async_copy(kernel_ref.at[:, p, q], held_ref.at[:, p, q], sems.at[3 * p + q])
            copy.start()
            copies.append(copy)
    return copies


def wait_all(copies):
    for copy in copies:
        copy.wait()


def fetch(pairs, sems):
    copies = [pltpu.make_async_copy(a, b, sems.at[i]) for i, (a, b) in enumerate(pairs)]
    for copy in copies:
        copy.start()
    return copies


def taps(kernel_ref, p, q):
    return jnp.concatenate([kernel_ref[s, p, q] for s in range(3)], axis=0)


def first_kernel(latents_ref, row_ref, copy_ref, first_ref, last_ref):
    value = latents_ref[...].astype(F32)
    copy_ref[...] = latents_ref[...]
    first_ref[...] = value[:, :, :1].astype(BF16)
    last_ref[...] = value[:, :, 15:].astype(BF16)
    row_ref[...] = own_stats(value.reshape(-1, value.shape[3]))


def edge_copy(ref, frames, pitch, rows, cols, edges):
    row_first, row_last, col_first, col_last = edges
    height = sum(rows)

    def copy(frame, to, source, size):
        ref[frame, to : to + size] = ref[frame, source : source + size]

    @pl.when(col_first)
    def _():
        for frame in range(frames):
            for row in range(height):
                for c in range(cols[0]):
                    copy(frame, row * pitch + c, row * pitch + cols[0], 1)

    @pl.when(col_last)
    def _():
        for frame in range(frames):
            for row in range(height):
                at = row * pitch + cols[0] + cols[1]
                for c in range(cols[2]):
                    copy(frame, at + c, at - 1, 1)

    @pl.when(row_first)
    def _():
        for frame in range(frames):
            for row in range(rows[0]):
                copy(frame, row * pitch, rows[0] * pitch, pitch)

    @pl.when(row_last)
    def _():
        end = rows[0] + rows[1]
        for frame in range(frames):
            for row in range(end, height):
                copy(frame, row * pitch, (end - 1) * pitch, pitch)


def strip_kernel(
    every_ref, wide_ref, wide1_ref, p2_ref, p3_ref, gain_ref, shift_ref, kernel_ref, offset_ref,
    row_ref, hidden_ref, act_ref,
):
    tm = lax.axis_index("tm")
    channels = gain_ref.shape[1]
    terms = (*norm_terms(every_ref[...], gain_ref[...], 4 * 512), shift_ref[...])
    rows = pl.ds(4 * tm, 10)
    for distance, piece_ref in enumerate((wide_ref.at[:, rows], wide1_ref.at[:, rows], p2_ref, p3_ref)):
        source = lax.rem(tm + 4 - distance, 4)
        for frame in range(2):
            for row in range(10):
                act_ref[2 * source + frame, row * WIDE : row * WIDE + WIDE] = norm_silu(
                    piece_ref[frame, row], *terms
                )
    size = 8 * WIDE
    for p in range(3):
        for pair in range(4):
            for q in range(3):
                start = p * WIDE + q
                rows = []
                for frame in (2 * pair, 2 * pair + 1):
                    parts = [
                        act_ref[max(frame + s - 2, 0), start : start + size].astype(BF16) for s in range(3)
                    ]
                    rows.append(jnp.concatenate(parts, axis=1))
                product = jnp.dot(
                    jnp.concatenate(rows, axis=0), taps(kernel_ref, p, q), preferred_element_type=F32
                ).reshape(2, size, channels)
                frames = slice(2 * pair, 2 * pair + 2)
                if p + q == 0:
                    hidden_ref[frames] = product + offset_ref[...]
                else:
                    hidden_ref[frames] += product
    own = [
        hidden_ref[frame, row * WIDE + 2 : row * WIDE + 18] for frame in range(8) for row in range(2, 6)
    ]
    own = jnp.concatenate(own, axis=0)
    row_ref[...] = own_stats(own)


def cut_kernel(
    given_ref, s0_ref, s1_ref, s2_ref, s3_ref, hidden_ref, cut_ref,
):
    tm, row_first, row_last, col_first, col_last = place()
    channels = hidden_ref.shape[2]
    hidden_ref[...] = given_ref[...]
    edges = (row_first & (tm == 0), row_last & (tm == 3), col_first, col_last)
    edge_copy(hidden_ref, 8, WIDE, (2, 4, 2), (2, 16, 2), edges)
    center = jnp.zeros((1, channels), F32)
    for frame in range(8):
        center = center + jnp.sum(hidden_ref[frame, 2 * WIDE : 6 * WIDE], axis=0, keepdims=True)
    center = center / (8 * 4 * WIDE)
    high = center.astype(BF16).astype(F32)
    low = (center - high).astype(BF16).astype(F32)
    center = high + low
    for frame in range(8):
        cut_ref[frame, 100:101] = high
        cut_ref[frame, 101:102] = low
        cut_ref[frame, 102:104] = jnp.zeros((2, channels), F32)
    for at in range(4):

        @pl.when(tm == at)
        def _(at=at):
            for frame in range(8):
                for row in range(5):
                    first = (at + row) * WIDE
                    cut_ref[frame, row * PITCH : row * PITCH + PITCH] = (
                        hidden_ref[frame, first : first + PITCH] - center
                    )

    for distance, part_ref in enumerate((s0_ref, s1_ref, s2_ref, s3_ref)):
        target = lax.rem(tm + distance, 4)
        parts = [cut_ref[jnp.maximum(2 * target - 4 + g, 0)] for g in range(6)]
        part_ref[...] = jnp.concatenate(parts, axis=0).astype(BF16)


def last_kernel(
    every_ref, s0_ref, s1_ref, s2_ref, s3_ref, far_before_ref, far_wide_ref, gain_ref, shift_ref, far_two_ref,
    offset_two_ref, far_three_ref, offset_three_ref,
    out_ref, act_ref, block_ref, part_ref, sum_ref, mix_ref, piece_ref, before_ref, wide_ref, kernel_two_ref,
    kernel_three_ref, piece_sems, two_sems, three_sems,
):
    tm, row_first, row_last, col_first, col_last = place()
    channels = gain_ref.shape[1]
    pieces = [(ref, piece_ref.at[d]) for d, ref in enumerate((s0_ref, s1_ref, s2_ref, s3_ref))]
    arrivals = fetch([*pieces, (far_before_ref, before_ref), (far_wide_ref, wide_ref)], piece_sems)
    kernels_two = fetch_taps(far_two_ref, kernel_two_ref, two_sems, (0,))
    mean, factor = norm_terms(every_ref[...], gain_ref[...], 4 * 512)
    wait_all(arrivals[:4])
    kernels_two += fetch_taps(far_two_ref, kernel_two_ref, two_sems, (1, 2))
    for source in range(4):
        held = piece_ref[lax.rem(tm + 4 - source, 4)].astype(F32)
        offset = (held[100:101] + held[101:102]) - mean
        for frame in range(6):
            value = held[frame * 104 : frame * 104 + 100] + offset
            act_ref[frame, source * 100 : source * 100 + 100] = norm_silu(value, 0.0, factor, shift_ref[...])
    wait_all(arrivals[4:])
    for frame in range(4):
        for row in range(18):
            own = wide_ref[max(frame - 2, 0), row + 2, 2:22].astype(F32)
            if frame < 2:
                own = jnp.where(tm == 0, own, before_ref[frame, row + 2, 2:22].astype(F32))
            block_ref[frame, row * PITCH : row * PITCH + PITCH] = own
    size = 18 * PITCH
    for p in range(3):
        wait_all(kernels_two[3 * p : 3 * p + 3])
        if p == 0:
            kernels_three = fetch_taps(far_three_ref, kernel_three_ref, three_sems, range(3))
        for pair in range(2):
            for q in range(3):
                rows = []
                for frame in (2 * pair, 2 * pair + 1):
                    start = p * PITCH + q
                    parts = [act_ref[frame + s, start : start + size] for s in range(3)]
                    rows.append(jnp.concatenate(parts, axis=1))
                product = jnp.dot(
                    jnp.concatenate(rows, axis=0).astype(BF16),
                    taps(kernel_two_ref, p, q),
                    preferred_element_type=F32,
                ).reshape(2, size, channels)
                if p + q == 0:
                    product = product + offset_two_ref[...]
                block_ref[2 * pair : 2 * pair + 2] += product
    edge_copy(block_ref, 4, PITCH, (1, 16, 1), (1, 16, 1), (row_first, row_last, col_first, col_last))
    rows = [
        jnp.concatenate([block_ref[frame + s] for s in range(3)], axis=1)
        for frame in range(2)
    ]
    wide = jnp.concatenate(rows, axis=0).astype(BF16)
    out_size = 16 * PITCH
    wait_all(kernels_three)
    for p in range(3):
        for q in range(3):
            part_ref[q, :, 0:size] = jnp.dot(
                wide, taps(kernel_three_ref, p, q), preferred_element_type=F32
            ).reshape(2, size, channels)
        middle = part_ref[1, :, 1 : 1 + size]
        sum_ref[p, 0] = part_ref[0, :, 0:size] + middle + part_ref[2, :, 1 : 1 + size]
        sum_ref[p, 1] = part_ref[0, :, 1 : 1 + size] + middle + part_ref[2, :, 2 : 2 + size]
    for frame in range(2):
        for half in range(channels // 128):
            lanes = slice(half * 128, half * 128 + 128)
            for b in range(2):
                middle = sum_ref[1, b, frame, PITCH : PITCH + out_size, lanes] + offset_three_ref[:, lanes]
                for a in range(2):
                    up = sum_ref[0, b, frame, a * PITCH : a * PITCH + out_size, lanes]
                    down = sum_ref[2, b, frame, (1 + a) * PITCH : (1 + a) * PITCH + out_size, lanes]
                    mix_ref[frame, half, a, pl.ds(b, out_size, stride=2), :] = up + middle + down
            for a in range(2):
                for i in range(16):
                    at = 2 * PITCH * i
                    out_ref[frame, 2 * i + a, :, lanes] = mix_ref[frame, half, a, at : at + 32].astype(BF16)


def run_kernel(body, name, in_specs, out_shape, scratch, flops, limit, *args):
    return pl.pallas_call(
        body,
        name=name,
        out_shape=out_shape,
        in_specs=in_specs,
        out_specs=jax.tree.map(lambda _: VMEM, out_shape),
        scratch_shapes=scratch,
        cost_estimate=pl.CostEstimate(flops=flops, bytes_accessed=8 * 2**20, transcendentals=0),
        compiler_params=pltpu.CompilerParams(vmem_limit_bytes=limit * 2**20),
    )(*args)


def held_taps(channels):
    return pltpu.VMEM((3, 3, 3, channels, channels), BF16)


def strip_call(every, wide, before, strips, gain, shift, kernel, offset):
    channels = wide.shape[3]
    return run_kernel(
        strip_kernel,
        "strip",
        [VMEM] * 9,
        (jax.ShapeDtypeStruct((8, 128), F32), jax.ShapeDtypeStruct((8, 8 * WIDE, channels), F32)),
        [pltpu.VMEM((8, 224, channels), F32)],
        2 * 1408 * 27 * channels * channels,
        24,
        every, wide, before, *strips, gain, shift, kernel, offset,
    )


def cut_call(hidden):
    channels = hidden.shape[2]
    part_shape = jax.ShapeDtypeStruct((624, channels), BF16)
    scratch = [pltpu.VMEM((8, 8 * WIDE, channels), F32), pltpu.VMEM((8, 104, channels), F32)]
    return run_kernel(cut_kernel, "cut", [VMEM], (part_shape,) * 4, scratch, 2**20, 16, hidden)


def last_call(every, parts, before, wide, gain, shift, kernel_two, offset_two, kernel_three, offset_three):
    channels = wide.shape[3]
    macs = 27 * channels * channels
    return run_kernel(
        last_kernel,
        "last",
        [VMEM] + [ANY] * 6 + [VMEM, VMEM, ANY, VMEM, ANY, VMEM],
        jax.ShapeDtypeStruct((2, 32, 32, channels), BF16),
        [
            pltpu.VMEM((6, 408, channels), F32),
            pltpu.VMEM((4, 18 * PITCH, channels), F32),
            pltpu.VMEM((3, 2, 19 * PITCH, channels), F32),
            pltpu.VMEM((3, 2, 2, 18 * PITCH, channels), F32),
            pltpu.VMEM((2, channels // 128, 2, 32 * PITCH, 128), F32),
            pltpu.VMEM((4, 624, channels), BF16),
            pltpu.VMEM((2, 22, WIDE, channels), BF16),
            pltpu.VMEM((2, 22, WIDE, channels), BF16),
            held_taps(channels),
            held_taps(channels),
            pltpu.SemaphoreType.DMA((6,)),
            pltpu.SemaphoreType.DMA((9,)),
            pltpu.SemaphoreType.DMA((9,)),
        ],
        2 * 2160 * macs,
        62,
        every, *parts, before, wide, gain, shift, kernel_two, offset_two, kernel_three, offset_three,
    )


def merged(rows):
    means = jnp.concatenate([row[:, :GROUPS] for row in rows])
    spreads = jnp.concatenate([row[:, GROUPS:] for row in rows])
    mean = jnp.mean(means, axis=0, keepdims=True)
    off = means - mean
    count = 512 * (256 // GROUPS)
    return jnp.concatenate(
        [mean, jnp.sum(spreads, axis=0, keepdims=True) + count * jnp.sum(off * off, axis=0, keepdims=True)],
        axis=1,
    )


def tm_rows(row):
    row = row[:1, :64]
    return [row] + [around(row, "tm", d) for d in (1, 2, 3)]


def repeated(row):
    row = jnp.concatenate([row, row], axis=1)
    peers = lax.axis_size("row") * lax.axis_size("col")
    return jnp.broadcast_to(row, (peers, row.shape[1]))


def exchanged(sent):
    return lax.all_to_all(sent, ("row", "col"), 0, 0, tiled=True)


def moved(value, axis, distance):
    devices = range(lax.axis_size(axis))
    return lax.ppermute(value, axis, [(i, i + distance) for i in devices if i + distance in devices])


def around(value, axis, distance):
    size = lax.axis_size(axis)
    return lax.ppermute(value, axis, [(i, (i + distance) % size) for i in range(size)])


def gathered(latents):
    _, row_first, row_last, col_first, col_last = place()
    left, right = moved(latents[:, :, 13:], "col", 1), moved(latents[:, :, :3], "col", -1)
    row_shape = jax.ShapeDtypeStruct((8, 128), F32)
    x_shape = jax.ShapeDtypeStruct(latents.shape, BF16)
    side_shape = jax.ShapeDtypeStruct((2, 16, 1, latents.shape[3]), BF16)
    row, x, first, last = run_kernel(
        first_kernel, "first", [VMEM], (row_shape, x_shape, side_shape, side_shape), [], 2**20, 8, latents
    )
    row, x, left, right = lax.optimization_barrier((row, x, left, right))
    left = jnp.where(col_first, first, left)
    right = jnp.where(col_last, last, right)
    x = jnp.concatenate([left, x, right], axis=2)
    top, bottom = moved(x[:, 13:], "row", 1), moved(x[:, :3], "row", -1)
    rows, x, top, bottom = lax.optimization_barrier((tm_rows(row), x, top, bottom))
    top = jnp.where(row_first, x[:, :1], top)
    bottom = jnp.where(row_last, x[:, 15:], bottom)
    return lax.optimization_barrier((merged(rows), jnp.concatenate([top, x, bottom], axis=1)))


def laid(value):
    return with_layout_constraint(value, Layout(tuple(range(value.ndim))))


def strip_of(wide, peer):
    return lax.dynamic_slice_in_dim(wide, 4 * peer, 10, axis=1)


def on_device(
    latents, gain_one, shift_one, kernel_one, offset_one, gain_two, shift_two, kernel_two, offset_two,
    kernel_three, offset_three,
):
    gain_one, shift_one, offset_one, gain_two, shift_two, offset_two, offset_three = (
        v[None] for v in (gain_one, shift_one, offset_one, gain_two, shift_two, offset_two, offset_three)
    )
    tm = lax.axis_index("tm")
    row, wide = gathered(latents)
    wide = laid(wide)
    before = laid(around(wide, "tm", 1))
    strips = [around(strip_of(wide, (tm + d) % 4), "tm", d) for d in (2, 3)]
    every = exchanged(repeated(row))
    row, hidden = strip_call(every, wide, before, strips, gain_one, shift_one, kernel_one, offset_one)
    sent = repeated(merged(tm_rows(row)))
    parts = cut_call(hidden)
    parts = [parts[0]] + [around(parts[d], "tm", d) for d in (1, 2, 3)]
    every = exchanged(sent)
    return last_call(
        every, parts, before, wide, gain_two, shift_two, kernel_two, offset_two, kernel_three, offset_three
    )


def solution(mesh):
    return jax.shard_map(
        on_device,
        mesh=mesh,
        in_specs=(P("tm", "row", "col", None), P(), P(), P(), P(), P(), P(), P(), P(), P(), P()),
        out_specs=P("tm", "row", "col", None),
        check_vma=False,
    )
```

profile of v0, /device:TPU:1, one launch (start us, length us, event | category | flops | bytes accessed | tf_op | source)
XLA Modules:
  0.0 99.2 jit_solution(16351166525396819479)
XLA Ops:
  0.0 1.1 %fusion.5 = (bf16[2,16,3,256]{3,2,1,0:T(4,128)(2,1)S(1)}, bf16[2,16,3,256]{3,2,1,0:T(4,128)(2,1)S(1)}) fusion(bf16[2,16,16,256]{3,2,1,0:T(8,128)(2,1)} %latents_ref.1), kind=kLoop, calls=%fused_computation.26 | loop fusion | bytes 196608 | tf_op jit(solution)/shard_map/slice | solution.py:417
  1.1 5.1 %collective-permute-start.1 = (bf16[2,16,3,256]{3,2,1,0:T(4,128)(2,1)S(1)}, bf16[2,16,3,256]{3,2,1,0:T(4,128)(2,1)S(1)}, u32[]{:S(2)}, u32[]{:S(2)}) collective-permute-start(bf16[2,16,3,256]{3,2,1,0:T(4,128)(2,1)S(1)} %get-tuple-element.57), channel_id=1, source_target_pairs={{1,0},{2,1},{3,2},{4,3},{5,4},{6,5},{7,6},{9,8},{10,9},{11,10},{12... | collective-permute-start | bytes 147464 | tf_op jit(solution)/shard_map/ppermute | solution.py:407
  6.2 1.9 %collective-permute-start = (bf16[2,16,3,256]{3,2,1,0:T(4,128)(2,1)S(1)}, bf16[2,16,3,256]{3,2,1,0:T(4,128)(2,1)S(1)}, u32[]{:S(2)}, u32[]{:S(2)}) collective-permute-start(bf16[2,16,3,256]{3,2,1,0:T(4,128)(2,1)S(1)} %get-tuple-element.58), channel_id=1, source_target_pairs={{0,1},{1,2},{2,3},{3,4},{4,5},{5,6},{6,7},{8,9},{9,10},{10,11},{11... | collective-permute-start | bytes 147464 | tf_op jit(solution)/shard_map/ppermute | solution.py:407
  8.2 0.0 copy-start.1
  8.2 0.9 copy-done.1
  9.1 0.8 first.1
  9.9 0.0 collective-permute-done.1
  10.0 0.0 collective-permute-done
  10.1 0.2 pad_maximum_fusion.1
  10.3 1.3 %collective-permute-start.6 = (bf16[2,3,22,256]{3,2,1,0:T(8,128)(2,1)S(1)}, bf16[2,3,22,256]{3,2,1,0:T(8,128)(2,1)S(1)}, u32[]{:S(2)}, u32[]{:S(2)}) collective-permute-start(bf16[2,3,22,256]{3,2,1,0:T(8,128)(2,1)S(1)} %get-tuple-element.55), channel_id=1, source_target_pairs={{8,0},{16,8},{24,16},{32,24},{40,32},{48,40},{56,48},{9,1},{17,9},... | collective-permute-start | bytes 202760 | tf_op jit(solution)/shard_map/ppermute | solution.py:407
  11.6 4.0 %collective-permute-start.5 = (bf16[2,3,22,256]{3,2,1,0:T(8,128)(2,1)S(1)}, bf16[2,3,22,256]{3,2,1,0:T(8,128)(2,1)S(1)}, u32[]{:S(2)}, u32[]{:S(2)}) collective-permute-start(bf16[2,3,22,256]{3,2,1,0:T(8,128)(2,1)S(1)} %get-tuple-element.56), channel_id=1, source_target_pairs={{0,8},{8,16},{16,24},{24,32},{32,40},{40,48},{48,56},{1,9},{9,17},... | collective-permute-start | bytes 202760 | tf_op jit(solution)/shard_map/ppermute | solution.py:407
  15.6 2.2 %collective-permute-start.4 = (f32[1,64]{1,0:T(1,128)S(1)}, f32[1,64]{1,0:T(1,128)S(1)}, u32[]{:S(2)}, u32[]{:S(2)}) collective-permute-start(f32[1,64]{1,0:T(1,128)S(1)} %slice.76), channel_id=1, source_target_pairs={{0,192},{64,0},{128,64},{192,128},{1,193},{65,1},{129,65},{193,129... | collective-permute-start | bytes 776 | tf_op jit(solution)/shard_map/ppermute | solution.py:412
  17.8 0.5 collective-permute-start.3
  18.4 0.6 collective-permute-start.2
  19.0 0.0 collective-permute-done.4
  19.0 2.8 %collective-permute-done.3 = f32[1,64]{1,0:T(1,128)S(1)} collective-permute-done((f32[1,64]{1,0:T(1,128)S(1)}, f32[1,64]{1,0:T(1,128)S(1)}, u32[]{:S(2)}, u32[]{:S(2)}) %collective-permute-start.3) | collective-permute-done | bytes 288 | tf_op jit(solution)/shard_map/ppermute | solution.py:412
  21.7 0.2 collective-permute-done.2
  22.0 0.0 collective-permute-done.6
  22.0 0.0 collective-permute-done.5
  22.0 0.1 bitcast_add_fusion.1
  22.1 0.1 pad_maximum_fusion.2
  22.2 0.1 pad_maximum_fusion.wide_ref.far_wide_ref
  22.3 0.0 copy-start
  22.3 0.4 copy.12
  22.7 0.1 collective-permute-start.7
  22.9 2.7 %collective-permute-start.9 = (bf16[2,10,22,256]{3,2,1,0:T(8,128)(2,1)S(1)}, bf16[2,10,22,256]{3,2,1,0:T(8,128)(2,1)S(1)}, u32[]{:S(2)}, u32[]{:S(2)}) collective-permute-start(bf16[2,10,22,256]{3,2,1,0:T(8,128)(2,1)S(1)} %get-tuple-element.51), channel_id=1, source_target_pairs={{0,192},{64,0},{128,64},{192,128},{1,193},{65,1},{129,65},{193,129... | collective-permute-start | bytes 675848 | tf_op jit(solution)/shard_map/ppermute | solution.py:412
  25.6 0.0 collective-permute-start.8
  25.6 0.1 maximum_bitcast_fusion
  25.7 0.6 broadcast_in_dim.79
  26.3 15.3 %all-to-all-start = ((f32[64,1,128]{2,1,0:T(1,128)}), f32[64,1,128]{2,1,0:T(1,128)S(1)}, u32[]{:S(2)}, u32[]{:S(2)}) async-start(f32[64,1,128]{2,1,0:T(1,128)} %broadcast_in_dim.79), calls=%async_computation | async-start | bytes 65536 | tf_op jit(solution)/shard_map/all_to_all | solution.py:402
  41.6 0.0 collective-permute-done.7
  41.6 0.1 copy.13.wide1_ref.far_before_ref
  41.6 0.0 copy-start.2
  41.7 9.2 %all-to-all-done = f32[64,1,128]{2,1,0:T(1,128)S(1)} async-done(((f32[64,1,128]{2,1,0:T(1,128)}), f32[64,1,128]{2,1,0:T(1,128)S(1)}, u32[]{:S(2)}, u32[]{:S(2)}) %all-to-all-start) | async-done | bytes 32800 | tf_op jit(solution)/shard_map/all_to_all | solution.py:402
  50.9 0.0 collective-permute-done.9.p3_ref
  50.9 0.0 collective-permute-done.8.p2_ref
  50.9 0.0 copy-done.7
  50.9 0.0 copy-done.6
  50.9 0.0 copy-done.5
  50.9 0.0 copy-start.3
  50.9 2.0 %copy-done.3 = bf16[3,3,3,256,256]{4,3,2,1,0:T(8,128)(2,1)S(1)} copy-done((bf16[3,3,3,256,256]{4,3,2,1,0:T(8,128)(2,1)S(1)}, bf16[3,3,3,256,256]{4,3,2,1,0:T(8,128)(2,1)}, u32[]{:S(2)}) %copy-start.3) | copy-done | bytes 3538968
  52.9 7.1 %strip.1 = (f32[8,128]{1,0:T(8,128)S(1)}, f32[8,176,256]{2,1,0:T(8,128)S(1)}) custom-call(f32[64,128]{1,0:T(8,128)S(1)} %bitcast.27, bf16[2,22,22,256]{3,2,1,0:T(8,128)(2,1)S(1)} %pad_maximum_fusion.wide_ref.far_wide_ref, bf16[2,22,22,256]{3,2,1,0:T(8,128)(2,1)S(1)} %copy.13.wide1_ref.far_before_ref, ...), custom_call_target="tpu_custom_call" | custom-call | flops 4982833152 | bytes 8388608 | tf_op jit(solution)/shard_map/strip/pallas_call | solution.py:312
  60.0 0.0 copy-done
  60.0 1.0 %collective-permute-start.12 = (f32[1,64]{1,0:T(1,128)S(1)}, f32[1,64]{1,0:T(1,128)S(1)}, u32[]{:S(2)}, u32[]{:S(2)}) collective-permute-start(f32[1,64]{1,0:T(1,128)S(1)} %slice.90), channel_id=1, source_target_pairs={{0,192},{64,0},{128,64},{192,128},{1,193},{65,1},{129,65},{193,129... | collective-permute-start | bytes 776 | tf_op jit(solution)/shard_map/ppermute | solution.py:412
  61.0 2.1 %collective-permute-start.11 = (f32[1,64]{1,0:T(1,128)S(1)}, f32[1,64]{1,0:T(1,128)S(1)}, u32[]{:S(2)}, u32[]{:S(2)}) collective-permute-start(f32[1,64]{1,0:T(1,128)S(1)} %slice.90), channel_id=1, source_target_pairs={{0,128},{64,192},{128,0},{192,64},{1,129},{65,193},{129,1},{193,65... | collective-permute-start | bytes 776 | tf_op jit(solution)/shard_map/ppermute | solution.py:412
  63.1 0.8 collective-permute-start.10
  63.9 0.5 cut.1
  64.4 0.7 copy-done.4
  65.1 0.0 collective-permute-start.13
  65.1 3.1 %collective-permute-start.14 = (bf16[624,256]{1,0:T(8,128)(2,1)S(1)}, bf16[624,256]{1,0:T(8,128)(2,1)S(1)}, u32[]{:S(2)}, u32[]{:S(2)}) collective-permute-start(bf16[624,256]{1,0:T(8,128)(2,1)S(1)} %get-tuple-element.49), channel_id=1, source_target_pairs={{0,128},{64,192},{128,0},{192,64},{1,129},{65,193},{129,1},{193,65... | collective-permute-start | bytes 958472 | tf_op jit(solution)/shard_map/ppermute | solution.py:412
  68.1 0.0 collective-permute-done.12
  68.1 0.2 collective-permute-start.15
  68.3 0.0 collective-permute-done.11
  68.4 0.0 collective-permute-done.10
  68.4 0.1 bitcast_add_fusion
  68.5 0.1 maximum_bitcast_fusion.1
  68.6 15.7 %all_to_all.16 = f32[64,1,128]{2,1,0:T(1,128)} all-to-all(f32[64,1,128]{2,1,0:T(1,128)S(1)} %broadcast_in_dim.83), channel_id=1, replica_groups=mesh['tm'=4,'row'=8,'col'=8] {'row','col'}, dimensions={0} | all-to-all | bytes 65536 | tf_op jit(solution)/shard_map/all_to_all | solution.py:402
  84.3 0.0 collective-permute-done.13.s1_ref
  84.3 0.0 collective-permute-done.14.s2_ref
  84.3 0.0 collective-permute-done.15.s3_ref
  84.3 0.7 copy-done.8
  85.0 0.1 copy-done.9
  85.1 0.1 copy-done.10
  85.2 13.8 %last.1 = bf16[2,32,32,256]{3,2,1,0:T(8,128)(2,1)} custom-call(f32[64,128]{1,0:T(8,128)} %bitcast.31, bf16[624,256]{1,0:T(8,128)(2,1)} %copy-done.4, bf16[624,256]{1,0:T(8,128)(2,1)} %copy-done.8, bf16[624,256]{1,0:T(8,128)(2,1)} %copy-done.9, bf16[624,256]{1,0:T(8,128)(2,1)} %copy-done.10, bf16[2,22,22,256]{3,2,1,0:T(8,128)(2,1)} %copy-done.2, ...), custom_call_target="tpu_custom_call" | custom-call | flops 7644119040 | bytes 8388608 | tf_op jit(solution)/shard_map/last/pallas_call | solution.py:312
  (23 shorter events, 0.3 us)
Async XLA Ops:
  0.0 50.9 %copy-start.7 = (f32[256]{0:T(256)S(1)}, f32[256]{0:T(256)}, u32[]{:S(2)}) copy-start(f32[256]{0:T(256)} %param.15) | copy-start | bytes 3076
  0.0 50.9 %copy-start.6 = (f32[256]{0:T(256)S(1)}, f32[256]{0:T(256)}, u32[]{:S(2)}) copy-start(f32[256]{0:T(256)} %param.13) | copy-start | bytes 3076
  0.0 50.9 %copy-start.5 = (f32[256]{0:T(256)S(1)}, f32[256]{0:T(256)}, u32[]{:S(2)}) copy-start(f32[256]{0:T(256)} %param.12) | copy-start | bytes 3076
  1.1 8.9 %collective-permute-start.1 = (bf16[2,16,3,256]{3,2,1,0:T(4,128)(2,1)S(1)}, bf16[2,16,3,256]{3,2,1,0:T(4,128)(2,1)S(1)}, u32[]{:S(2)}, u32[]{:S(2)}) collective-permute-start(bf16[2,16,3,256]{3,2,1,0:T(4,128)(2,1)S(1)} %get-tuple-element.57), channel_id=1, source_target_pairs={{1,0},{2,1},{3,2},{4,3},{5,4},{6,5},{7,6},{9,8},{10,9},{11,10},{12... | collective-permute-start | bytes 147464 | tf_op jit(solution)/shard_map/ppermute | solution.py:407
  6.2 3.7 %collective-permute-start = (bf16[2,16,3,256]{3,2,1,0:T(4,128)(2,1)S(1)}, bf16[2,16,3,256]{3,2,1,0:T(4,128)(2,1)S(1)}, u32[]{:S(2)}, u32[]{:S(2)}) collective-permute-start(bf16[2,16,3,256]{3,2,1,0:T(4,128)(2,1)S(1)} %get-tuple-element.58), channel_id=1, source_target_pairs={{0,1},{1,2},{2,3},{3,4},{4,5},{5,6},{6,7},{8,9},{9,10},{10,11},{11... | collective-permute-start | bytes 147464 | tf_op jit(solution)/shard_map/ppermute | solution.py:407
  8.2 1.0 copy-start.1
  10.3 11.6 %collective-permute-start.6 = (bf16[2,3,22,256]{3,2,1,0:T(8,128)(2,1)S(1)}, bf16[2,3,22,256]{3,2,1,0:T(8,128)(2,1)S(1)}, u32[]{:S(2)}, u32[]{:S(2)}) collective-permute-start(bf16[2,3,22,256]{3,2,1,0:T(8,128)(2,1)S(1)} %get-tuple-element.55), channel_id=1, source_target_pairs={{8,0},{16,8},{24,16},{32,24},{40,32},{48,40},{56,48},{9,1},{17,9},... | collective-permute-start | bytes 202760 | tf_op jit(solution)/shard_map/ppermute | solution.py:407
  11.6 10.3 %collective-permute-start.5 = (bf16[2,3,22,256]{3,2,1,0:T(8,128)(2,1)S(1)}, bf16[2,3,22,256]{3,2,1,0:T(8,128)(2,1)S(1)}, u32[]{:S(2)}, u32[]{:S(2)}) collective-permute-start(bf16[2,3,22,256]{3,2,1,0:T(8,128)(2,1)S(1)} %get-tuple-element.56), channel_id=1, source_target_pairs={{0,8},{8,16},{16,24},{24,32},{32,40},{40,48},{48,56},{1,9},{9,17},... | collective-permute-start | bytes 202760 | tf_op jit(solution)/shard_map/ppermute | solution.py:407
  15.6 3.3 %collective-permute-start.4 = (f32[1,64]{1,0:T(1,128)S(1)}, f32[1,64]{1,0:T(1,128)S(1)}, u32[]{:S(2)}, u32[]{:S(2)}) collective-permute-start(f32[1,64]{1,0:T(1,128)S(1)} %slice.76), channel_id=1, source_target_pairs={{0,192},{64,0},{128,64},{192,128},{1,193},{65,1},{129,65},{193,129... | collective-permute-start | bytes 776 | tf_op jit(solution)/shard_map/ppermute | solution.py:412
  17.8 3.9 %collective-permute-start.3 = (f32[1,64]{1,0:T(1,128)S(1)}, f32[1,64]{1,0:T(1,128)S(1)}, u32[]{:S(2)}, u32[]{:S(2)}) collective-permute-start(f32[1,64]{1,0:T(1,128)S(1)} %slice.76), channel_id=1, source_target_pairs={{0,128},{64,192},{128,0},{192,64},{1,129},{65,193},{129,1},{193,65... | collective-permute-start | bytes 776 | tf_op jit(solution)/shard_map/ppermute | solution.py:412
  18.4 3.6 %collective-permute-start.2 = (f32[1,64]{1,0:T(1,128)S(1)}, f32[1,64]{1,0:T(1,128)S(1)}, u32[]{:S(2)}, u32[]{:S(2)}) collective-permute-start(f32[1,64]{1,0:T(1,128)S(1)} %slice.76), channel_id=1, source_target_pairs={{0,64},{64,128},{128,192},{192,0},{1,65},{65,129},{129,193},{193,1... | collective-permute-start | bytes 776 | tf_op jit(solution)/shard_map/ppermute | solution.py:412
  22.3 37.7 %copy-start = (bf16[2,22,22,256]{3,2,1,0:T(8,128)(2,1)}, bf16[2,22,22,256]{3,2,1,0:T(8,128)(2,1)S(1)}, u32[]{:S(2)}) copy-start(bf16[2,22,22,256]{3,2,1,0:T(8,128)(2,1)S(1)} %pad_maximum_fusion.wide_ref.far_wide_ref) | copy-start | bytes 1486852
  22.7 18.9 %collective-permute-start.7 = (bf16[2,22,22,256]{3,0,2,1:T(2,128)(2,1)S(1)}, bf16[2,22,22,256]{3,0,2,1:T(2,128)(2,1)S(1)}, u32[]{:S(2)}, u32[]{:S(2)}) collective-permute-start(bf16[2,22,22,256]{3,0,2,1:T(2,128)(2,1)S(1)} %copy.12), channel_id=1, source_target_pairs={{0,64},{64,128},{128,192},{192,0},{1,65},{65,129},{129,193},{193,1... | collective-permute-start | bytes 1486856 | tf_op jit(solution)/shard_map/ppermute | solution.py:412
  22.9 28.0 %collective-permute-start.9 = (bf16[2,10,22,256]{3,2,1,0:T(8,128)(2,1)S(1)}, bf16[2,10,22,256]{3,2,1,0:T(8,128)(2,1)S(1)}, u32[]{:S(2)}, u32[]{:S(2)}) collective-permute-start(bf16[2,10,22,256]{3,2,1,0:T(8,128)(2,1)S(1)} %get-tuple-element.51), channel_id=1, source_target_pairs={{0,192},{64,0},{128,64},{192,128},{1,193},{65,1},{129,65},{193,129... | collective-permute-start | bytes 675848 | tf_op jit(solution)/shard_map/ppermute | solution.py:412
  25.6 25.3 %collective-permute-start.8 = (bf16[2,10,22,256]{3,2,1,0:T(8,128)(2,1)S(1)}, bf16[2,10,22,256]{3,2,1,0:T(8,128)(2,1)S(1)}, u32[]{:S(2)}, u32[]{:S(2)}) collective-permute-start(bf16[2,10,22,256]{3,2,1,0:T(8,128)(2,1)S(1)} %get-tuple-element.52), channel_id=1, source_target_pairs={{0,128},{64,192},{128,0},{192,64},{1,129},{65,193},{129,1},{193,65... | collective-permute-start | bytes 675848 | tf_op jit(solution)/shard_map/ppermute | solution.py:412
  26.3 24.6 %all-to-all-start = ((f32[64,1,128]{2,1,0:T(1,128)}), f32[64,1,128]{2,1,0:T(1,128)S(1)}, u32[]{:S(2)}, u32[]{:S(2)}) async-start(f32[64,1,128]{2,1,0:T(1,128)} %broadcast_in_dim.79), calls=%async_computation | async-start | bytes 65536 | tf_op jit(solution)/shard_map/all_to_all | solution.py:402
  41.6 18.3 %copy-start.2 = (bf16[2,22,22,256]{3,2,1,0:T(8,128)(2,1)}, bf16[2,22,22,256]{3,2,1,0:T(8,128)(2,1)S(1)}, u32[]{:S(2)}) copy-start(bf16[2,22,22,256]{3,2,1,0:T(8,128)(2,1)S(1)} %copy.13.wide1_ref.far_before_ref) | copy-start | bytes 1486852
  50.9 2.0 %copy-start.3 = (bf16[3,3,3,256,256]{4,3,2,1,0:T(8,128)(2,1)S(1)}, bf16[3,3,3,256,256]{4,3,2,1,0:T(8,128)(2,1)}, u32[]{:S(2)}) copy-start(bf16[3,3,3,256,256]{4,3,2,1,0:T(8,128)(2,1)} %kernel_ref.1) | copy-start | bytes 10616836
  60.0 8.1 %collective-permute-start.12 = (f32[1,64]{1,0:T(1,128)S(1)}, f32[1,64]{1,0:T(1,128)S(1)}, u32[]{:S(2)}, u32[]{:S(2)}) collective-permute-start(f32[1,64]{1,0:T(1,128)S(1)} %slice.90), channel_id=1, source_target_pairs={{0,192},{64,0},{128,64},{192,128},{1,193},{65,1},{129,65},{193,129... | collective-permute-start | bytes 776 | tf_op jit(solution)/shard_map/ppermute | solution.py:412
  61.0 7.3 %collective-permute-start.11 = (f32[1,64]{1,0:T(1,128)S(1)}, f32[1,64]{1,0:T(1,128)S(1)}, u32[]{:S(2)}, u32[]{:S(2)}) collective-permute-start(f32[1,64]{1,0:T(1,128)S(1)} %slice.90), channel_id=1, source_target_pairs={{0,128},{64,192},{128,0},{192,64},{1,129},{65,193},{129,1},{193,65... | collective-permute-start | bytes 776 | tf_op jit(solution)/shard_map/ppermute | solution.py:412
  63.1 5.2 %collective-permute-start.10 = (f32[1,64]{1,0:T(1,128)S(1)}, f32[1,64]{1,0:T(1,128)S(1)}, u32[]{:S(2)}, u32[]{:S(2)}) collective-permute-start(f32[1,64]{1,0:T(1,128)S(1)} %slice.90), channel_id=1, source_target_pairs={{0,64},{64,128},{128,192},{192,0},{1,65},{65,129},{129,193},{193,1... | collective-permute-start | bytes 776 | tf_op jit(solution)/shard_map/ppermute | solution.py:412
  64.3 0.7 copy-start.4
  65.1 19.2 %collective-permute-start.13 = (bf16[624,256]{1,0:T(8,128)(2,1)S(1)}, bf16[624,256]{1,0:T(8,128)(2,1)S(1)}, u32[]{:S(2)}, u32[]{:S(2)}) collective-permute-start(bf16[624,256]{1,0:T(8,128)(2,1)S(1)} %get-tuple-element.48), channel_id=1, source_target_pairs={{0,64},{64,128},{128,192},{192,0},{1,65},{65,129},{129,193},{193,1... | collective-permute-start | bytes 958472 | tf_op jit(solution)/shard_map/ppermute | solution.py:412
  65.1 19.2 %collective-permute-start.14 = (bf16[624,256]{1,0:T(8,128)(2,1)S(1)}, bf16[624,256]{1,0:T(8,128)(2,1)S(1)}, u32[]{:S(2)}, u32[]{:S(2)}) collective-permute-start(bf16[624,256]{1,0:T(8,128)(2,1)S(1)} %get-tuple-element.49), channel_id=1, source_target_pairs={{0,128},{64,192},{128,0},{192,64},{1,129},{65,193},{129,1},{193,65... | collective-permute-start | bytes 958472 | tf_op jit(solution)/shard_map/ppermute | solution.py:412
  68.1 16.2 %collective-permute-start.15 = (bf16[624,256]{1,0:T(8,128)(2,1)S(1)}, bf16[624,256]{1,0:T(8,128)(2,1)S(1)}, u32[]{:S(2)}, u32[]{:S(2)}) collective-permute-start(bf16[624,256]{1,0:T(8,128)(2,1)S(1)} %get-tuple-element.50), channel_id=1, source_target_pairs={{0,192},{64,0},{128,64},{192,128},{1,193},{65,1},{129,65},{193,129... | collective-permute-start | bytes 958472 | tf_op jit(solution)/shard_map/ppermute | solution.py:412
  84.3 0.7 copy-start.8
  84.3 0.8 copy-start.9
  84.3 0.9 copy-start.10
where the time goes:
time: 99.6 us; the launch traced here: 99.2 us
  starting transfers between devices  40.9 us (41%)
  Pallas kernels  22.1 us (22%)
  blocking collectives  15.7 us (16%)
  waiting for transfers between devices  12.2 us (12%)
  local copies, waits for them, and re-layouts  6.87 us (7%)
    pallas_call x4, Pallas kernels, run_kernel(): pl.pallas_call(body, name=name, out_shape=out_shape, in_specs=in_specs, o...  22.1 us
    all_to_all x1, blocking collectives, exchanged(): return lax.all_to_all(sent, ('row', 'col'), 0, 0, tiled=True)  15.7 us
    all_to_all x1, starting transfers between devices, exchanged(): return lax.all_to_all(sent, ('row', 'col'), 0, 0, tiled=True)  15.3 us
    ppermute x12, starting transfers between devices, around(): lax.ppermute(value, axis, [(i, (i + distance) % size) for i in range(size)])  13.3 us
    ppermute x4, starting transfers between devices, moved(): lax.ppermute(value, axis, [(i, i + distance) for i in devices if i + dist...  12.4 us
    all_to_all x1, waiting for transfers between devices, exchanged(): return lax.all_to_all(sent, ('row', 'col'), 0, 0, tiled=True)  9.19 us
    unnamed x23, local copies, waits for them, and re-layouts  4.62 us
    ppermute x12, waiting for transfers between devices, around(): lax.ppermute(value, axis, [(i, (i + distance) % size) for i in range(size)])  3.02 us
  transfers between devices with their start and end apart: 17, of which 3 were waited for; matrix products, arithmetic and copies ran while one was open for 1% of the time, Pallas kernels for 1%

commit v1 on v0

--- a/solution.py
+++ b/solution.py
@@ -2,7 +2,6 @@
 import jax.numpy as jnp
 from jax import lax
 from jax.experimental import pallas as pl
-from jax.experimental.layout import Layout, with_layout_constraint
 from jax.experimental.pallas import tpu as pltpu
 from jax.sharding import PartitionSpec as P
 
@@ -18,7 +17,14 @@
 
 
 def exact_dot(a, b):
-    return jnp.dot(a, b, precision=lax.Precision.HIGHEST, preferred_element_type=F32)
+    high = a.astype(BF16)
+    rest = a - high.astype(F32)
+    middle = rest.astype(BF16)
+    low = (rest - middle.astype(F32)).astype(BF16)
+    parts = [part.astype(F32) for part in (high, middle, low)]
+    stacked = jnp.concatenate([*parts, jnp.zeros_like(a)], axis=0).astype(BF16)
+    product = jnp.dot(stacked, b.astype(BF16), preferred_element_type=F32)
+    return product[:8] + (product[8:16] + product[16:24])
 
 
 def iotas(shape):
@@ -30,24 +36,26 @@
     return (lane % 64 == channel // (channels // GROUPS) + first).astype(F32)
 
 
-def channel_to_lane(channels):
-    channel, lane = iotas((channels, 128))
-    return (lane % GROUPS == channel // (channels // GROUPS)).astype(F32)
-
-
 def eight(row):
     return jnp.broadcast_to(row, (8, row.shape[1]))
 
 
 def own_stats(flat):
     rows, channels = flat.shape
-    to_lane = channel_to_lane(channels)
-    count = rows * (channels // GROUPS)
-    mean = exact_dot(eight(jnp.sum(flat, axis=0, keepdims=True)), to_lane) / count
-    own_mean = exact_dot(jnp.where(iotas(mean.shape)[1] < 64, mean, 0.0), lane_to_channel(0, channels))
-    centered = flat - own_mean[:1]
-    spread = exact_dot(eight(jnp.sum(centered * centered, axis=0, keepdims=True)), to_lane)
-    return jnp.where(iotas(mean.shape)[1] % 64 < GROUPS, mean, spread)
+    width = channels // GROUPS
+    mean = eight(jnp.sum(flat, axis=0, keepdims=True)) / rows
+    centered = flat - mean[:1]
+    spread = eight(jnp.sum(centered * centered, axis=0, keepdims=True))
+    left, right = iotas((channels, channels))
+    group_mean = exact_dot(mean, (left // width == right // width).astype(F32)) / width
+    off = mean - group_mean
+    spread = spread + rows * off * off
+    channel, lane = iotas((channels, 128))
+    own = (lane % GROUPS == channel // width).astype(F32)
+    first = own * (channel % width == 0).astype(F32)
+    both = jnp.where(iotas(mean.shape)[0] < 4, group_mean, spread)
+    means, spreads = exact_dot(both, first), exact_dot(both, own)
+    return jnp.where(iotas(means.shape)[1] % 64 < GROUPS, eight(means[:1]), eight(spreads[7:]))
 
 
 def norm_terms(every, gain, cells):
@@ -432,10 +440,6 @@
     return lax.optimization_barrier((merged(rows), jnp.concatenate([top, x, bottom], axis=1)))
 
 
-def laid(value):
-    return with_layout_constraint(value, Layout(tuple(range(value.ndim))))
-
-
 def strip_of(wide, peer):
     return lax.dynamic_slice_in_dim(wide, 4 * peer, 10, axis=1)
 
@@ -449,8 +453,7 @@
     )
     tm = lax.axis_index("tm")
     row, wide = gathered(latents)
-    wide = laid(wide)
-    before = laid(around(wide, "tm", 1))
+    before = around(wide.reshape(44, WIDE, -1), "tm", 1).reshape(wide.shape)
     strips = [around(strip_of(wide, (tm + d) % 4), "tm", d) for d in (2, 3)]
     every = exchanged(repeated(row))
     row, hidden = strip_call(every, wide, before, strips, gain_one, shift_one, kernel_one, offset_one)

time: 99.6 us -> 98.2 us (0.986)
  blocking collectives: 15.7 us -> 40.6 us
  starting transfers between devices: 40.9 us -> 25.6 us
  waiting for transfers between devices: 12.2 us -> 3.03 us
  Pallas kernels: 22.1 us -> 21.1 us
    all_to_all x1 -> x2, blocking collectives: 15.7 us -> 40.6 us  [exchanged(): return lax.all_to_all(sent, ('row', 'col'), 0, 0, tiled=True)]
    all_to_all x1 -> x0, starting transfers between devices: 15.3 us -> none  [exchanged(): return lax.all_to_all(sent, ('row', 'col'), 0, 0, tiled=True)]
    all_to_all x1 -> x0, waiting for transfers between devices: 9.19 us -> none  [exchanged(): return lax.all_to_all(sent, ('row', 'col'), 0, 0, tiled=True)]
  transfers between devices with their start and end apart: 17 -> 16, of which waited for: 3 -> 2; matrix products, arithmetic and copies ran while one was open for 1% -> 0% of each run, Pallas kernels for 1% -> 1%
where the time goes in v1:
time: 98.2 us; the launch traced here: 97.8 us
  blocking collectives  40.6 us (41%)
  starting transfers between devices  25.6 us (26%)
  Pallas kernels  21.1 us (21%)
  local copies, waits for them, and re-layouts  5.97 us (6%)
  waiting for transfers between devices  3.03 us (3%)
    all_to_all x2, blocking collectives, exchanged(): return lax.all_to_all(sent, ('row', 'col'), 0, 0, tiled=True)  40.6 us
    pallas_call x4, Pallas kernels, run_kernel(): pl.pallas_call(body, name=name, out_shape=out_shape, in_specs=in_specs, o...  21.1 us
    ppermute x12, starting transfers between devices, around(): lax.ppermute(value, axis, [(i, (i + distance) % size) for i in range(size)])  13.3 us
    ppermute x4, starting transfers between devices, moved(): lax.ppermute(value, axis, [(i, i + distance) for i in devices if i + dist...  12.4 us
    unnamed x23, local copies, waits for them, and re-layouts  4.8 us
    ppermute x12, waiting for transfers between devices, around(): lax.ppermute(value, axis, [(i, (i + distance) % size) for i in range(size)])  3.02 us
  transfers between devices with their start and end apart: 16, of which 2 were waited for; matrix products, arithmetic and copies ran while one was open for 0% of the time, Pallas kernels for 1%

profile of v1, /device:TPU:1, one launch (start us, length us, event | category | flops | bytes accessed | tf_op | source)
XLA Modules:
  0.0 97.8 jit_solution(7086962308633402263)
XLA Ops:
  0.0 1.1 %fusion.5 = (bf16[2,16,3,256]{3,2,1,0:T(4,128)(2,1)S(1)}, bf16[2,16,3,256]{3,2,1,0:T(4,128)(2,1)S(1)}) fusion(bf16[2,16,16,256]{3,2,1,0:T(8,128)(2,1)} %latents_ref.1), kind=kLoop, calls=%fused_computation.26 | loop fusion | bytes 196608 | tf_op jit(solution)/shard_map/slice | solution.py:425
  1.1 5.1 %collective-permute-start.1 = (bf16[2,16,3,256]{3,2,1,0:T(4,128)(2,1)S(1)}, bf16[2,16,3,256]{3,2,1,0:T(4,128)(2,1)S(1)}, u32[]{:S(2)}, u32[]{:S(2)}) collective-permute-start(bf16[2,16,3,256]{3,2,1,0:T(4,128)(2,1)S(1)} %get-tuple-element.57), channel_id=1, source_target_pairs={{1,0},{2,1},{3,2},{4,3},{5,4},{6,5},{7,6},{9,8},{10,9},{11,10},{12... | collective-permute-start | bytes 147464 | tf_op jit(solution)/shard_map/ppermute | solution.py:415
  6.2 1.9 %collective-permute-start = (bf16[2,16,3,256]{3,2,1,0:T(4,128)(2,1)S(1)}, bf16[2,16,3,256]{3,2,1,0:T(4,128)(2,1)S(1)}, u32[]{:S(2)}, u32[]{:S(2)}) collective-permute-start(bf16[2,16,3,256]{3,2,1,0:T(4,128)(2,1)S(1)} %get-tuple-element.58), channel_id=1, source_target_pairs={{0,1},{1,2},{2,3},{3,4},{4,5},{5,6},{6,7},{8,9},{9,10},{10,11},{11... | collective-permute-start | bytes 147464 | tf_op jit(solution)/shard_map/ppermute | solution.py:415
  8.2 0.0 copy-start.1
  8.2 0.9 copy-done.1
  9.1 0.4 first.1
  9.6 0.0 collective-permute-done.1
  9.6 0.0 collective-permute-done
  9.7 0.2 pad_maximum_fusion.1
  10.0 1.3 %collective-permute-start.6 = (bf16[2,3,22,256]{3,2,1,0:T(8,128)(2,1)S(1)}, bf16[2,3,22,256]{3,2,1,0:T(8,128)(2,1)S(1)}, u32[]{:S(2)}, u32[]{:S(2)}) collective-permute-start(bf16[2,3,22,256]{3,2,1,0:T(8,128)(2,1)S(1)} %get-tuple-element.55), channel_id=1, source_target_pairs={{8,0},{16,8},{24,16},{32,24},{40,32},{48,40},{56,48},{9,1},{17,9},... | collective-permute-start | bytes 202760 | tf_op jit(solution)/shard_map/ppermute | solution.py:415
  11.3 4.0 %collective-permute-start.5 = (bf16[2,3,22,256]{3,2,1,0:T(8,128)(2,1)S(1)}, bf16[2,3,22,256]{3,2,1,0:T(8,128)(2,1)S(1)}, u32[]{:S(2)}, u32[]{:S(2)}) collective-permute-start(bf16[2,3,22,256]{3,2,1,0:T(8,128)(2,1)S(1)} %get-tuple-element.56), channel_id=1, source_target_pairs={{0,8},{8,16},{16,24},{24,32},{32,40},{40,48},{48,56},{1,9},{9,17},... | collective-permute-start | bytes 202760 | tf_op jit(solution)/shard_map/ppermute | solution.py:415
  15.3 2.2 %collective-permute-start.4 = (f32[1,64]{1,0:T(1,128)S(1)}, f32[1,64]{1,0:T(1,128)S(1)}, u32[]{:S(2)}, u32[]{:S(2)}) collective-permute-start(f32[1,64]{1,0:T(1,128)S(1)} %slice.76), channel_id=1, source_target_pairs={{0,192},{64,0},{128,64},{192,128},{1,193},{65,1},{129,65},{193,129... | collective-permute-start | bytes 776 | tf_op jit(solution)/shard_map/ppermute | solution.py:420
  17.5 0.5 collective-permute-start.3
  18.0 0.6 collective-permute-start.2
  18.6 0.0 collective-permute-done.4
  18.6 2.8 %collective-permute-done.3 = f32[1,64]{1,0:T(1,128)S(1)} collective-permute-done((f32[1,64]{1,0:T(1,128)S(1)}, f32[1,64]{1,0:T(1,128)S(1)}, u32[]{:S(2)}, u32[]{:S(2)}) %collective-permute-start.3) | collective-permute-done | bytes 288 | tf_op jit(solution)/shard_map/ppermute | solution.py:420
  21.3 0.2 collective-permute-done.2
  21.6 0.0 collective-permute-done.6
  21.6 0.0 collective-permute-done.5
  21.6 0.1 bitcast_add_fusion.1
  21.7 0.1 pad_maximum_fusion.2
  21.8 0.1 pad_maximum_fusion.wide_ref.far_wide_ref
  21.9 0.0 copy-start
  21.9 0.1 collective-permute-start.7
  22.1 2.7 %collective-permute-start.9 = (bf16[2,10,22,256]{3,2,1,0:T(8,128)(2,1)S(1)}, bf16[2,10,22,256]{3,2,1,0:T(8,128)(2,1)S(1)}, u32[]{:S(2)}, u32[]{:S(2)}) collective-permute-start(bf16[2,10,22,256]{3,2,1,0:T(8,128)(2,1)S(1)} %get-tuple-element.51), channel_id=1, source_target_pairs={{0,192},{64,0},{128,64},{192,128},{1,193},{65,1},{129,65},{193,129... | collective-permute-start | bytes 675848 | tf_op jit(solution)/shard_map/ppermute | solution.py:420
  24.8 0.0 collective-permute-start.8
  24.8 0.1 maximum_bitcast_fusion
  24.9 24.9 %all_to_all.16 = f32[64,1,128]{2,1,0:T(1,128)S(1)} all-to-all(f32[64,1,128]{2,1,0:T(1,128)S(1)} %broadcast_in_dim.79), channel_id=1, replica_groups=mesh['tm'=4,'row'=8,'col'=8] {'row','col'}, dimensions={0} | all-to-all | bytes 65536 | tf_op jit(solution)/shard_map/all_to_all | solution.py:410
  49.8 0.0 collective-permute-done.9.p3_ref
  49.8 0.0 collective-permute-done.8.p2_ref
  49.8 0.0 collective-permute-done.7
  49.8 0.0 copy-start.3
  49.8 0.0 copy-done.7
  49.8 0.0 copy-done.6
  49.8 0.0 copy-done.5
  49.8 0.0 copy-start.2
  49.8 2.2 %copy-done.2 = bf16[3,3,3,256,256]{4,3,2,1,0:T(8,128)(2,1)S(1)} copy-done((bf16[3,3,3,256,256]{4,3,2,1,0:T(8,128)(2,1)S(1)}, bf16[3,3,3,256,256]{4,3,2,1,0:T(8,128)(2,1)}, u32[]{:S(2)}) %copy-start.2) | copy-done | bytes 3538968
  52.0 6.5 %strip.1 = (f32[8,128]{1,0:T(8,128)S(1)}, f32[8,176,256]{2,1,0:T(8,128)S(1)}) custom-call(f32[64,128]{1,0:T(8,128)S(1)} %bitcast.30, bf16[2,22,22,256]{3,2,1,0:T(8,128)(2,1)S(1)} %pad_maximum_fusion.wide_ref.far_wide_ref, bf16[2,22,22,256]{3,2,1,0:T(8,128)(2,1)S(1)} %bitcast.31, bf16[2,10,22,256]{3,2,1,0:T(8,128)(2,1)S(1)} %collective-permute-done.8.p2_ref, ...), custom_call_target="tpu_custom_call" | custom-call | flops 4982833152 | bytes 8388608 | tf_op jit(solution)/shard_map/strip/pallas_call | solution.py:320
  58.5 0.0 copy-done
  58.5 0.0 copy-done.3
  58.5 1.0 collective-permute-start.12
  59.5 2.1 %collective-permute-start.11 = (f32[1,64]{1,0:T(1,128)S(1)}, f32[1,64]{1,0:T(1,128)S(1)}, u32[]{:S(2)}, u32[]{:S(2)}) collective-permute-start(f32[1,64]{1,0:T(1,128)S(1)} %slice.90), channel_id=1, source_target_pairs={{0,128},{64,192},{128,0},{192,64},{1,129},{65,193},{129,1},{193,65... | collective-permute-start | bytes 776 | tf_op jit(solution)/shard_map/ppermute | solution.py:420
  61.6 0.8 collective-permute-start.10
  62.3 0.5 cut.1
  62.8 0.0 copy-start.4
  62.8 0.7 copy-done.4
  63.5 0.0 collective-permute-start.13
  63.5 3.1 %collective-permute-start.14 = (bf16[624,256]{1,0:T(8,128)(2,1)S(1)}, bf16[624,256]{1,0:T(8,128)(2,1)S(1)}, u32[]{:S(2)}, u32[]{:S(2)}) collective-permute-start(bf16[624,256]{1,0:T(8,128)(2,1)S(1)} %get-tuple-element.49), channel_id=1, source_target_pairs={{0,128},{64,192},{128,0},{192,64},{1,129},{65,193},{129,1},{193,65... | collective-permute-start | bytes 958472 | tf_op jit(solution)/shard_map/ppermute | solution.py:420
  66.6 0.0 collective-permute-done.12
  66.6 0.3 collective-permute-start.15
  66.9 0.0 collective-permute-done.11
  66.9 0.0 collective-permute-done.10
  66.9 0.1 bitcast_add_fusion
  67.0 0.1 maximum_bitcast_fusion.1
  67.1 15.8 %all_to_all.17 = f32[64,1,128]{2,1,0:T(1,128)} all-to-all(f32[64,1,128]{2,1,0:T(1,128)S(1)} %broadcast_in_dim.83), channel_id=1, replica_groups=mesh['tm'=4,'row'=8,'col'=8] {'row','col'}, dimensions={0} | all-to-all | bytes 65536 | tf_op jit(solution)/shard_map/all_to_all | solution.py:410
  82.8 0.0 collective-permute-done.13.s1_ref
  82.9 0.0 collective-permute-done.14.s2_ref
  82.9 0.0 copy-start.9
  82.9 0.0 collective-permute-done.15.s3_ref
  82.9 0.0 copy-start.10
  82.9 0.7 copy-done.8
  83.6 0.1 copy-done.9
  83.7 0.1 copy-done.10
  83.8 13.8 %last.1 = bf16[2,32,32,256]{3,2,1,0:T(8,128)(2,1)} custom-call(f32[64,128]{1,0:T(8,128)} %bitcast.36, bf16[624,256]{1,0:T(8,128)(2,1)} %copy-done.4, bf16[624,256]{1,0:T(8,128)(2,1)} %copy-done.8, bf16[624,256]{1,0:T(8,128)(2,1)} %copy-done.9, bf16[624,256]{1,0:T(8,128)(2,1)} %copy-done.10, bf16[2,22,22,256]{3,2,1,0:T(8,128)(2,1)} %bitcast.32, ...), custom_call_target="tpu_custom_call" | custom-call | flops 7644119040 | bytes 8388608 | tf_op jit(solution)/shard_map/last/pallas_call | solution.py:320
  (20 shorter events, 0.3 us)
Async XLA Ops:
  0.0 49.8 %copy-start.7 = (f32[256]{0:T(256)S(1)}, f32[256]{0:T(256)}, u32[]{:S(2)}) copy-start(f32[256]{0:T(256)} %param.15) | copy-start | bytes 3076
  0.0 49.8 %copy-start.6 = (f32[256]{0:T(256)S(1)}, f32[256]{0:T(256)}, u32[]{:S(2)}) copy-start(f32[256]{0:T(256)} %param.13) | copy-start | bytes 3076
  0.0 49.8 %copy-start.5 = (f32[256]{0:T(256)S(1)}, f32[256]{0:T(256)}, u32[]{:S(2)}) copy-start(f32[256]{0:T(256)} %param.12) | copy-start | bytes 3076
  1.1 8.5 %collective-permute-start.1 = (bf16[2,16,3,256]{3,2,1,0:T(4,128)(2,1)S(1)}, bf16[2,16,3,256]{3,2,1,0:T(4,128)(2,1)S(1)}, u32[]{:S(2)}, u32[]{:S(2)}) collective-permute-start(bf16[2,16,3,256]{3,2,1,0:T(4,128)(2,1)S(1)} %get-tuple-element.57), channel_id=1, source_target_pairs={{1,0},{2,1},{3,2},{4,3},{5,4},{6,5},{7,6},{9,8},{10,9},{11,10},{12... | collective-permute-start | bytes 147464 | tf_op jit(solution)/shard_map/ppermute | solution.py:415
  6.2 3.4 %collective-permute-start = (bf16[2,16,3,256]{3,2,1,0:T(4,128)(2,1)S(1)}, bf16[2,16,3,256]{3,2,1,0:T(4,128)(2,1)S(1)}, u32[]{:S(2)}, u32[]{:S(2)}) collective-permute-start(bf16[2,16,3,256]{3,2,1,0:T(4,128)(2,1)S(1)} %get-tuple-element.58), channel_id=1, source_target_pairs={{0,1},{1,2},{2,3},{3,4},{4,5},{5,6},{6,7},{8,9},{9,10},{10,11},{11... | collective-permute-start | bytes 147464 | tf_op jit(solution)/shard_map/ppermute | solution.py:415
  8.2 1.0 copy-start.1
  10.0 11.6 %collective-permute-start.6 = (bf16[2,3,22,256]{3,2,1,0:T(8,128)(2,1)S(1)}, bf16[2,3,22,256]{3,2,1,0:T(8,128)(2,1)S(1)}, u32[]{:S(2)}, u32[]{:S(2)}) collective-permute-start(bf16[2,3,22,256]{3,2,1,0:T(8,128)(2,1)S(1)} %get-tuple-element.55), channel_id=1, source_target_pairs={{8,0},{16,8},{24,16},{32,24},{40,32},{48,40},{56,48},{9,1},{17,9},... | collective-permute-start | bytes 202760 | tf_op jit(solution)/shard_map/ppermute | solution.py:415
  11.3 10.3 %collective-permute-start.5 = (bf16[2,3,22,256]{3,2,1,0:T(8,128)(2,1)S(1)}, bf16[2,3,22,256]{3,2,1,0:T(8,128)(2,1)S(1)}, u32[]{:S(2)}, u32[]{:S(2)}) collective-permute-start(bf16[2,3,22,256]{3,2,1,0:T(8,128)(2,1)S(1)} %get-tuple-element.56), channel_id=1, source_target_pairs={{0,8},{8,16},{16,24},{24,32},{32,40},{40,48},{48,56},{1,9},{9,17},... | collective-permute-start | bytes 202760 | tf_op jit(solution)/shard_map/ppermute | solution.py:415
  15.3 3.3 %collective-permute-start.4 = (f32[1,64]{1,0:T(1,128)S(1)}, f32[1,64]{1,0:T(1,128)S(1)}, u32[]{:S(2)}, u32[]{:S(2)}) collective-permute-start(f32[1,64]{1,0:T(1,128)S(1)} %slice.76), channel_id=1, source_target_pairs={{0,192},{64,0},{128,64},{192,128},{1,193},{65,1},{129,65},{193,129... | collective-permute-start | bytes 776 | tf_op jit(solution)/shard_map/ppermute | solution.py:420
  17.5 3.9 %collective-permute-start.3 = (f32[1,64]{1,0:T(1,128)S(1)}, f32[1,64]{1,0:T(1,128)S(1)}, u32[]{:S(2)}, u32[]{:S(2)}) collective-permute-start(f32[1,64]{1,0:T(1,128)S(1)} %slice.76), channel_id=1, source_target_pairs={{0,128},{64,192},{128,0},{192,64},{1,129},{65,193},{129,1},{193,65... | collective-permute-start | bytes 776 | tf_op jit(solution)/shard_map/ppermute | solution.py:420
  18.0 3.6 %collective-permute-start.2 = (f32[1,64]{1,0:T(1,128)S(1)}, f32[1,64]{1,0:T(1,128)S(1)}, u32[]{:S(2)}, u32[]{:S(2)}) collective-permute-start(f32[1,64]{1,0:T(1,128)S(1)} %slice.76), channel_id=1, source_target_pairs={{0,64},{64,128},{128,192},{192,0},{1,65},{65,129},{129,193},{193,1... | collective-permute-start | bytes 776 | tf_op jit(solution)/shard_map/ppermute | solution.py:420
  21.9 36.6 %copy-start = (bf16[2,22,22,256]{3,2,1,0:T(8,128)(2,1)}, bf16[2,22,22,256]{3,2,1,0:T(8,128)(2,1)S(1)}, u32[]{:S(2)}) copy-start(bf16[2,22,22,256]{3,2,1,0:T(8,128)(2,1)S(1)} %pad_maximum_fusion.wide_ref.far_wide_ref) | copy-start | bytes 1486852
  21.9 27.9 %collective-permute-start.7 = (bf16[44,22,256]{2,1,0:T(8,128)(2,1)S(1)}, bf16[44,22,256]{2,1,0:T(8,128)(2,1)S(1)}, u32[]{:S(2)}, u32[]{:S(2)}) collective-permute-start(bf16[44,22,256]{2,1,0:T(8,128)(2,1)S(1)} %bitcast.29), channel_id=1, source_target_pairs={{0,64},{64,128},{128,192},{192,0},{1,65},{65,129},{129,193},{193,1... | collective-permute-start | bytes 1486856 | tf_op jit(solution)/shard_map/ppermute | solution.py:420
  22.1 27.7 %collective-permute-start.9 = (bf16[2,10,22,256]{3,2,1,0:T(8,128)(2,1)S(1)}, bf16[2,10,22,256]{3,2,1,0:T(8,128)(2,1)S(1)}, u32[]{:S(2)}, u32[]{:S(2)}) collective-permute-start(bf16[2,10,22,256]{3,2,1,0:T(8,128)(2,1)S(1)} %get-tuple-element.51), channel_id=1, source_target_pairs={{0,192},{64,0},{128,64},{192,128},{1,193},{65,1},{129,65},{193,129... | collective-permute-start | bytes 675848 | tf_op jit(solution)/shard_map/ppermute | solution.py:420
  24.8 25.0 %collective-permute-start.8 = (bf16[2,10,22,256]{3,2,1,0:T(8,128)(2,1)S(1)}, bf16[2,10,22,256]{3,2,1,0:T(8,128)(2,1)S(1)}, u32[]{:S(2)}, u32[]{:S(2)}) collective-permute-start(bf16[2,10,22,256]{3,2,1,0:T(8,128)(2,1)S(1)} %get-tuple-element.52), channel_id=1, source_target_pairs={{0,128},{64,192},{128,0},{192,64},{1,129},{65,193},{129,1},{193,65... | collective-permute-start | bytes 675848 | tf_op jit(solution)/shard_map/ppermute | solution.py:420
  49.8 8.7 %copy-start.3 = (bf16[44,22,256]{2,1,0:T(8,128)(2,1)}, bf16[44,22,256]{2,1,0:T(8,128)(2,1)S(1)}, u32[]{:S(2)}) copy-start(bf16[44,22,256]{2,1,0:T(8,128)(2,1)S(1)} %collective-permute-done.7) | copy-start | bytes 1486852
  49.8 2.2 %copy-start.2 = (bf16[3,3,3,256,256]{4,3,2,1,0:T(8,128)(2,1)S(1)}, bf16[3,3,3,256,256]{4,3,2,1,0:T(8,128)(2,1)}, u32[]{:S(2)}) copy-start(bf16[3,3,3,256,256]{4,3,2,1,0:T(8,128)(2,1)} %kernel_ref.1) | copy-start | bytes 10616836
  58.5 8.1 %collective-permute-start.12 = (f32[1,64]{1,0:T(1,128)S(1)}, f32[1,64]{1,0:T(1,128)S(1)}, u32[]{:S(2)}, u32[]{:S(2)}) collective-permute-start(f32[1,64]{1,0:T(1,128)S(1)} %slice.90), channel_id=1, source_target_pairs={{0,192},{64,0},{128,64},{192,128},{1,193},{65,1},{129,65},{193,129... | collective-permute-start | bytes 776 | tf_op jit(solution)/shard_map/ppermute | solution.py:420
  59.5 7.4 %collective-permute-start.11 = (f32[1,64]{1,0:T(1,128)S(1)}, f32[1,64]{1,0:T(1,128)S(1)}, u32[]{:S(2)}, u32[]{:S(2)}) collective-permute-start(f32[1,64]{1,0:T(1,128)S(1)} %slice.90), channel_id=1, source_target_pairs={{0,128},{64,192},{128,0},{192,64},{1,129},{65,193},{129,1},{193,65... | collective-permute-start | bytes 776 | tf_op jit(solution)/shard_map/ppermute | solution.py:420
  61.6 5.3 %collective-permute-start.10 = (f32[1,64]{1,0:T(1,128)S(1)}, f32[1,64]{1,0:T(1,128)S(1)}, u32[]{:S(2)}, u32[]{:S(2)}) collective-permute-start(f32[1,64]{1,0:T(1,128)S(1)} %slice.90), channel_id=1, source_target_pairs={{0,64},{64,128},{128,192},{192,0},{1,65},{65,129},{129,193},{193,1... | collective-permute-start | bytes 776 | tf_op jit(solution)/shard_map/ppermute | solution.py:420
  62.8 0.7 copy-start.4
  63.5 19.3 %collective-permute-start.13 = (bf16[624,256]{1,0:T(8,128)(2,1)S(1)}, bf16[624,256]{1,0:T(8,128)(2,1)S(1)}, u32[]{:S(2)}, u32[]{:S(2)}) collective-permute-start(bf16[624,256]{1,0:T(8,128)(2,1)S(1)} %get-tuple-element.48), channel_id=1, source_target_pairs={{0,64},{64,128},{128,192},{192,0},{1,65},{65,129},{129,193},{193,1... | collective-permute-start | bytes 958472 | tf_op jit(solution)/shard_map/ppermute | solution.py:420
  63.5 19.3 %collective-permute-start.14 = (bf16[624,256]{1,0:T(8,128)(2,1)S(1)}, bf16[624,256]{1,0:T(8,128)(2,1)S(1)}, u32[]{:S(2)}, u32[]{:S(2)}) collective-permute-start(bf16[624,256]{1,0:T(8,128)(2,1)S(1)} %get-tuple-element.49), channel_id=1, source_target_pairs={{0,128},{64,192},{128,0},{192,64},{1,129},{65,193},{129,1},{193,65... | collective-permute-start | bytes 958472 | tf_op jit(solution)/shard_map/ppermute | solution.py:420
  66.6 16.3 %collective-permute-start.15 = (bf16[624,256]{1,0:T(8,128)(2,1)S(1)}, bf16[624,256]{1,0:T(8,128)(2,1)S(1)}, u32[]{:S(2)}, u32[]{:S(2)}) collective-permute-start(bf16[624,256]{1,0:T(8,128)(2,1)S(1)} %get-tuple-element.50), channel_id=1, source_target_pairs={{0,192},{64,0},{128,64},{192,128},{1,193},{65,1},{129,65},{193,129... | collective-permute-start | bytes 958472 | tf_op jit(solution)/shard_map/ppermute | solution.py:420
  82.9 0.7 copy-start.8
  82.9 0.8 copy-start.9
  82.9 1.0 copy-start.10

commit v2 on v1

--- a/solution.py
+++ b/solution.py
@@ -434,10 +434,10 @@
     right = jnp.where(col_last, last, right)
     x = jnp.concatenate([left, x, right], axis=2)
     top, bottom = moved(x[:, 13:], "row", 1), moved(x[:, :3], "row", -1)
-    rows, x, top, bottom = lax.optimization_barrier((tm_rows(row), x, top, bottom))
+    rows = tm_rows(row)
     top = jnp.where(row_first, x[:, :1], top)
     bottom = jnp.where(row_last, x[:, 15:], bottom)
-    return lax.optimization_barrier((merged(rows), jnp.concatenate([top, x, bottom], axis=1)))
+    return merged(rows), jnp.concatenate([top, x, bottom], axis=1)
 
 
 def strip_of(wide, peer):

time: 98.2 us -> 96.8 us (0.986)
  local copies, waits for them, and re-layouts: 5.97 us -> 3.75 us
  blocking collectives: 40.6 us -> 39.2 us
  waiting for transfers between devices: 3.03 us -> 4.34 us
    ppermute x4, waiting for transfers between devices: 0.01 us -> 4.31 us  [moved(): lax.ppermute(value, axis, [(i, i + distance) for i in devices if i + dist...]
    ppermute x12, waiting for transfers between devices: 3.02 us -> 0.03 us  [around(): lax.ppermute(value, axis, [(i, (i + distance) % size) for i in range(size)])]
    unnamed x23, local copies, waits for them, and re-layouts: 4.8 us -> 2.65 us
    all_to_all x2, blocking collectives: 40.6 us -> 39.2 us  [exchanged(): return lax.all_to_all(sent, ('row', 'col'), 0, 0, tiled=True)]
    ppermute x12, starting transfers between devices: 13.3 us -> 14.3 us  [around(): lax.ppermute(value, axis, [(i, (i + distance) % size) for i in range(size)])]
  transfers between devices with their start and end apart: 16 -> 16, of which waited for: 2 -> 1; matrix products, arithmetic and copies ran while one was open for 0% -> 1% of each run, Pallas kernels for 1% -> 1%
where the time goes in v2:
time: 96.8 us; the launch traced here: 96.4 us
  blocking collectives  39.2 us (40%)
  starting transfers between devices  26.5 us (27%)
  Pallas kernels  21.1 us (22%)
  waiting for transfers between devices  4.34 us (4%)
  local copies, waits for them, and re-layouts  3.75 us (4%)
    all_to_all x2, blocking collectives, exchanged(): return lax.all_to_all(sent, ('row', 'col'), 0, 0, tiled=True)  39.2 us
    pallas_call x4, Pallas kernels, run_kernel(): pl.pallas_call(body, name=name, out_shape=out_shape, in_specs=in_specs, o...  21.1 us
    ppermute x12, starting transfers between devices, around(): lax.ppermute(value, axis, [(i, (i + distance) % size) for i in range(size)])  14.3 us
    ppermute x4, starting transfers between devices, moved(): lax.ppermute(value, axis, [(i, i + distance) for i in devices if i + dist...  12.2 us
    ppermute x4, waiting for transfers between devices, moved(): lax.ppermute(value, axis, [(i, i + distance) for i in devices if i + dist...  4.31 us
    unnamed x23, local copies, waits for them, and re-layouts  2.65 us
  transfers between devices with their start and end apart: 16, of which 1 were waited for; matrix products, arithmetic and copies ran while one was open for 1% of the time, Pallas kernels for 1%

profile of v2, /device:TPU:1, one launch (start us, length us, event | category | flops | bytes accessed | tf_op | source)
XLA Modules:
  0.0 96.4 jit_solution(11373365901554582618)
XLA Ops:
  0.0 1.0 %fusion.4 = (bf16[2,16,3,256]{3,2,1,0:T(4,128)(2,1)S(1)}, bf16[2,16,3,256]{3,2,1,0:T(4,128)(2,1)S(1)}) fusion(bf16[2,16,16,256]{3,2,1,0:T(8,128)(2,1)} %latents_ref.1), kind=kLoop, calls=%fused_computation.26 | loop fusion | bytes 196608 | tf_op jit(solution)/shard_map/slice | solution.py:425
  1.0 5.1 %collective-permute-start.1 = (bf16[2,16,3,256]{3,2,1,0:T(4,128)(2,1)S(1)}, bf16[2,16,3,256]{3,2,1,0:T(4,128)(2,1)S(1)}, u32[]{:S(2)}, u32[]{:S(2)}) collective-permute-start(bf16[2,16,3,256]{3,2,1,0:T(4,128)(2,1)S(1)} %get-tuple-element.39), channel_id=1, source_target_pairs={{1,0},{2,1},{3,2},{4,3},{5,4},{6,5},{7,6},{9,8},{10,9},{11,10},{12... | collective-permute-start | bytes 147464 | tf_op jit(solution)/shard_map/ppermute | solution.py:415
  6.2 1.9 %collective-permute-start = (bf16[2,16,3,256]{3,2,1,0:T(4,128)(2,1)S(1)}, bf16[2,16,3,256]{3,2,1,0:T(4,128)(2,1)S(1)}, u32[]{:S(2)}, u32[]{:S(2)}) collective-permute-start(bf16[2,16,3,256]{3,2,1,0:T(4,128)(2,1)S(1)} %get-tuple-element.40), channel_id=1, source_target_pairs={{0,1},{1,2},{2,3},{3,4},{4,5},{5,6},{6,7},{8,9},{9,10},{10,11},{11... | collective-permute-start | bytes 147464 | tf_op jit(solution)/shard_map/ppermute | solution.py:415
  8.1 0.0 copy-start.1
  8.1 0.9 copy-done.1
  9.1 0.4 first.1
  9.6 0.0 collective-permute-done.1
  9.6 0.0 collective-permute-done
  9.6 2.0 %collective-permute-start.4 = (f32[1,64]{1,0:T(1,128)S(1)}, f32[1,64]{1,0:T(1,128)S(1)}, u32[]{:S(2)}, u32[]{:S(2)}) collective-permute-start(f32[1,64]{1,0:T(1,128)S(1)} %slice.79), channel_id=1, source_target_pairs={{0,192},{64,0},{128,64},{192,128},{1,193},{65,1},{129,65},{193,129... | collective-permute-start | bytes 776 | tf_op jit(solution)/shard_map/ppermute | solution.py:420
  11.6 0.5 collective-permute-start.3
  12.1 0.6 collective-permute-start.2
  12.8 0.0 copy-start.5
  12.8 0.0 copy-start.6
  12.8 0.0 copy-start.7
  12.8 0.0 copy-start.2
  12.9 0.1 pad_maximum_fusion.3
  13.0 3.8 %collective-permute-start.5 = (bf16[2,3,22,256]{3,2,1,0:T(8,128)(2,1)S(1)}, bf16[2,3,22,256]{3,2,1,0:T(8,128)(2,1)S(1)}, u32[]{:S(2)}, u32[]{:S(2)}) collective-permute-start(bf16[2,3,22,256]{3,2,1,0:T(8,128)(2,1)S(1)} %get-tuple-element.37), channel_id=1, source_target_pairs={{0,8},{8,16},{16,24},{24,32},{32,40},{40,48},{48,56},{1,9},{9,17},... | collective-permute-start | bytes 202760 | tf_op jit(solution)/shard_map/ppermute | solution.py:415
  16.8 1.3 %collective-permute-start.6 = (bf16[2,3,22,256]{3,2,1,0:T(8,128)(2,1)S(1)}, bf16[2,3,22,256]{3,2,1,0:T(8,128)(2,1)S(1)}, u32[]{:S(2)}, u32[]{:S(2)}) collective-permute-start(bf16[2,3,22,256]{3,2,1,0:T(8,128)(2,1)S(1)} %get-tuple-element.38), channel_id=1, source_target_pairs={{8,0},{16,8},{24,16},{32,24},{40,32},{48,40},{56,48},{9,1},{17,9},... | collective-permute-start | bytes 202760 | tf_op jit(solution)/shard_map/ppermute | solution.py:415
  18.1 0.0 collective-permute-done.4
  18.1 0.0 collective-permute-done.3
  18.1 0.0 collective-permute-done.2
  18.2 0.0 collective-permute-done.5
  18.2 4.3 %collective-permute-done.6 = bf16[2,3,22,256]{3,2,1,0:T(8,128)(2,1)S(1)} collective-permute-done((bf16[2,3,22,256]{3,2,1,0:T(8,128)(2,1)S(1)}, bf16[2,3,22,256]{3,2,1,0:T(8,128)(2,1)S(1)}, u32[]{:S(2)}, u32[]{:S(2)}) %collective-permute-start.6) | collective-permute-done | bytes 67616 | tf_op jit(solution)/shard_map/ppermute | solution.py:415
  22.5 0.3 pad_maximum_fusion.wide_ref.far_wide_ref
  22.8 0.0 copy-start
  22.8 1.6 %collective-permute-start.7 = (bf16[44,22,256]{2,1,0:T(8,128)(2,1)S(1)}, bf16[44,22,256]{2,1,0:T(8,128)(2,1)S(1)}, u32[]{:S(2)}, u32[]{:S(2)}) collective-permute-start(bf16[44,22,256]{2,1,0:T(8,128)(2,1)S(1)} %bitcast.29), channel_id=1, source_target_pairs={{0,64},{64,128},{128,192},{192,0},{1,65},{65,129},{129,193},{193,1... | collective-permute-start | bytes 1486856 | tf_op jit(solution)/shard_map/ppermute | solution.py:420
  24.4 1.2 %collective-permute-start.9 = (bf16[2,10,22,256]{3,2,1,0:T(8,128)(2,1)S(1)}, bf16[2,10,22,256]{3,2,1,0:T(8,128)(2,1)S(1)}, u32[]{:S(2)}, u32[]{:S(2)}) collective-permute-start(bf16[2,10,22,256]{3,2,1,0:T(8,128)(2,1)S(1)} %get-tuple-element.33), channel_id=1, source_target_pairs={{0,192},{64,0},{128,64},{192,128},{1,193},{65,1},{129,65},{193,129... | collective-permute-start | bytes 675848 | tf_op jit(solution)/shard_map/ppermute | solution.py:420
  25.7 1.0 collective-permute-start.8
  26.6 0.1 bitcast_add_fusion.1
  26.7 0.1 maximum_bitcast_fusion.2
  26.8 23.6 %all_to_all.16 = f32[64,1,128]{2,1,0:T(1,128)S(1)} all-to-all(f32[64,1,128]{2,1,0:T(1,128)S(1)} %broadcast_in_dim.71), channel_id=1, replica_groups=mesh['tm'=4,'row'=8,'col'=8] {'row','col'}, dimensions={0} | all-to-all | bytes 65536 | tf_op jit(solution)/shard_map/all_to_all | solution.py:410
  50.4 0.0 collective-permute-done.9.p3_ref
  50.4 0.0 collective-permute-done.8.p2_ref
  50.4 0.0 collective-permute-done.7
  50.4 0.0 copy-start.3
  50.4 0.0 copy-done.5
  50.4 0.0 copy-done.6
  50.4 0.0 copy-done.7
  50.4 0.0 copy-done.2
  50.4 6.5 %strip.1 = (f32[8,128]{1,0:T(8,128)S(1)}, f32[8,176,256]{2,1,0:T(8,128)S(1)}) custom-call(f32[64,128]{1,0:T(8,128)S(1)} %bitcast.30, bf16[2,22,22,256]{3,2,1,0:T(8,128)(2,1)S(1)} %pad_maximum_fusion.wide_ref.far_wide_ref, bf16[2,22,22,256]{3,2,1,0:T(8,128)(2,1)S(1)} %bitcast.31, bf16[2,10,22,256]{3,2,1,0:T(8,128)(2,1)S(1)} %collective-permute-done.8.p2_ref, ...), custom_call_target="tpu_custom_call" | custom-call | flops 4982833152 | bytes 8388608 | tf_op jit(solution)/shard_map/strip/pallas_call | solution.py:320
  56.9 0.0 copy-done
  56.9 2.4 %collective-permute-start.12 = (f32[1,64]{1,0:T(1,128)S(1)}, f32[1,64]{1,0:T(1,128)S(1)}, u32[]{:S(2)}, u32[]{:S(2)}) collective-permute-start(f32[1,64]{1,0:T(1,128)S(1)} %slice.92), channel_id=1, source_target_pairs={{0,192},{64,0},{128,64},{192,128},{1,193},{65,1},{129,65},{193,129... | collective-permute-start | bytes 776 | tf_op jit(solution)/shard_map/ppermute | solution.py:420
  59.3 0.5 collective-permute-start.11
  59.8 0.6 collective-permute-start.10
  60.5 0.5 cut.1
  60.9 0.0 copy-start.4
  60.9 0.7 copy-done.4
  61.6 1.5 %collective-permute-start.13 = (bf16[624,256]{1,0:T(8,128)(2,1)S(1)}, bf16[624,256]{1,0:T(8,128)(2,1)S(1)}, u32[]{:S(2)}, u32[]{:S(2)}) collective-permute-start(bf16[624,256]{1,0:T(8,128)(2,1)S(1)} %get-tuple-element.30), channel_id=1, source_target_pairs={{0,64},{64,128},{128,192},{192,0},{1,65},{65,129},{129,193},{193,1... | collective-permute-start | bytes 958472 | tf_op jit(solution)/shard_map/ppermute | solution.py:420
  63.2 1.7 %collective-permute-start.14 = (bf16[624,256]{1,0:T(8,128)(2,1)S(1)}, bf16[624,256]{1,0:T(8,128)(2,1)S(1)}, u32[]{:S(2)}, u32[]{:S(2)}) collective-permute-start(bf16[624,256]{1,0:T(8,128)(2,1)S(1)} %get-tuple-element.31), channel_id=1, source_target_pairs={{0,128},{64,192},{128,0},{192,64},{1,129},{65,193},{129,1},{193,65... | collective-permute-start | bytes 958472 | tf_op jit(solution)/shard_map/ppermute | solution.py:420
  64.9 0.0 collective-permute-done.12
  64.9 0.7 collective-permute-start.15
  65.6 0.0 collective-permute-done.11
  65.6 0.0 collective-permute-done.10
  65.6 0.1 bitcast_add_fusion
  65.7 0.1 maximum_bitcast_fusion.3
  65.8 15.7 %all_to_all.17 = f32[64,1,128]{2,1,0:T(1,128)} all-to-all(f32[64,1,128]{2,1,0:T(1,128)S(1)} %broadcast_in_dim.83), channel_id=1, replica_groups=mesh['tm'=4,'row'=8,'col'=8] {'row','col'}, dimensions={0} | all-to-all | bytes 65536 | tf_op jit(solution)/shard_map/all_to_all | solution.py:410
  81.5 0.0 collective-permute-done.13.s1_ref
  81.5 0.0 collective-permute-done.14.s2_ref
  81.5 0.0 collective-permute-done.15.s3_ref
  81.5 0.0 copy-start.10
  81.5 0.7 copy-done.8
  82.2 0.1 copy-done.9
  82.3 0.1 copy-done.10
  82.4 13.8 %last.1 = bf16[2,32,32,256]{3,2,1,0:T(8,128)(2,1)} custom-call(f32[64,128]{1,0:T(8,128)} %bitcast.36, bf16[624,256]{1,0:T(8,128)(2,1)} %copy-done.4, bf16[624,256]{1,0:T(8,128)(2,1)} %copy-done.8, bf16[624,256]{1,0:T(8,128)(2,1)} %copy-done.9, bf16[624,256]{1,0:T(8,128)(2,1)} %copy-done.10, bf16[2,22,22,256]{3,2,1,0:T(8,128)(2,1)} %bitcast.32, ...), custom_call_target="tpu_custom_call" | custom-call | flops 7644119040 | bytes 8388608 | tf_op jit(solution)/shard_map/last/pallas_call | solution.py:320
  (18 shorter events, 0.3 us)
Async XLA Ops:
  1.0 8.5 %collective-permute-start.1 = (bf16[2,16,3,256]{3,2,1,0:T(4,128)(2,1)S(1)}, bf16[2,16,3,256]{3,2,1,0:T(4,128)(2,1)S(1)}, u32[]{:S(2)}, u32[]{:S(2)}) collective-permute-start(bf16[2,16,3,256]{3,2,1,0:T(4,128)(2,1)S(1)} %get-tuple-element.39), channel_id=1, source_target_pairs={{1,0},{2,1},{3,2},{4,3},{5,4},{6,5},{7,6},{9,8},{10,9},{11,10},{12... | collective-permute-start | bytes 147464 | tf_op jit(solution)/shard_map/ppermute | solution.py:415
  6.2 3.4 %collective-permute-start = (bf16[2,16,3,256]{3,2,1,0:T(4,128)(2,1)S(1)}, bf16[2,16,3,256]{3,2,1,0:T(4,128)(2,1)S(1)}, u32[]{:S(2)}, u32[]{:S(2)}) collective-permute-start(bf16[2,16,3,256]{3,2,1,0:T(4,128)(2,1)S(1)} %get-tuple-element.40), channel_id=1, source_target_pairs={{0,1},{1,2},{2,3},{3,4},{4,5},{5,6},{6,7},{8,9},{9,10},{10,11},{11... | collective-permute-start | bytes 147464 | tf_op jit(solution)/shard_map/ppermute | solution.py:415
  8.1 1.0 copy-start.1
  9.6 8.5 %collective-permute-start.4 = (f32[1,64]{1,0:T(1,128)S(1)}, f32[1,64]{1,0:T(1,128)S(1)}, u32[]{:S(2)}, u32[]{:S(2)}) collective-permute-start(f32[1,64]{1,0:T(1,128)S(1)} %slice.79), channel_id=1, source_target_pairs={{0,192},{64,0},{128,64},{192,128},{1,193},{65,1},{129,65},{193,129... | collective-permute-start | bytes 776 | tf_op jit(solution)/shard_map/ppermute | solution.py:420
  11.6 6.5 %collective-permute-start.3 = (f32[1,64]{1,0:T(1,128)S(1)}, f32[1,64]{1,0:T(1,128)S(1)}, u32[]{:S(2)}, u32[]{:S(2)}) collective-permute-start(f32[1,64]{1,0:T(1,128)S(1)} %slice.79), channel_id=1, source_target_pairs={{0,128},{64,192},{128,0},{192,64},{1,129},{65,193},{129,1},{193,65... | collective-permute-start | bytes 776 | tf_op jit(solution)/shard_map/ppermute | solution.py:420
  12.1 6.0 %collective-permute-start.2 = (f32[1,64]{1,0:T(1,128)S(1)}, f32[1,64]{1,0:T(1,128)S(1)}, u32[]{:S(2)}, u32[]{:S(2)}) collective-permute-start(f32[1,64]{1,0:T(1,128)S(1)} %slice.79), channel_id=1, source_target_pairs={{0,64},{64,128},{128,192},{192,0},{1,65},{65,129},{129,193},{193,1... | collective-permute-start | bytes 776 | tf_op jit(solution)/shard_map/ppermute | solution.py:420
  12.8 37.6 %copy-start.5 = (f32[256]{0:T(256)S(1)}, f32[256]{0:T(256)}, u32[]{:S(2)}) copy-start(f32[256]{0:T(256)} %param.12) | copy-start | bytes 3076
  12.8 37.6 %copy-start.6 = (f32[256]{0:T(256)S(1)}, f32[256]{0:T(256)}, u32[]{:S(2)}) copy-start(f32[256]{0:T(256)} %param.13) | copy-start | bytes 3076
  12.8 37.6 %copy-start.7 = (f32[256]{0:T(256)S(1)}, f32[256]{0:T(256)}, u32[]{:S(2)}) copy-start(f32[256]{0:T(256)} %param.15) | copy-start | bytes 3076
  12.8 37.6 %copy-start.2 = (bf16[3,3,3,256,256]{4,3,2,1,0:T(8,128)(2,1)S(1)}, bf16[3,3,3,256,256]{4,3,2,1,0:T(8,128)(2,1)}, u32[]{:S(2)}) copy-start(bf16[3,3,3,256,256]{4,3,2,1,0:T(8,128)(2,1)} %kernel_ref.1) | copy-start | bytes 10616836
  13.0 5.2 %collective-permute-start.5 = (bf16[2,3,22,256]{3,2,1,0:T(8,128)(2,1)S(1)}, bf16[2,3,22,256]{3,2,1,0:T(8,128)(2,1)S(1)}, u32[]{:S(2)}, u32[]{:S(2)}) collective-permute-start(bf16[2,3,22,256]{3,2,1,0:T(8,128)(2,1)S(1)} %get-tuple-element.37), channel_id=1, source_target_pairs={{0,8},{8,16},{16,24},{24,32},{32,40},{40,48},{48,56},{1,9},{9,17},... | collective-permute-start | bytes 202760 | tf_op jit(solution)/shard_map/ppermute | solution.py:415
  16.8 5.7 %collective-permute-start.6 = (bf16[2,3,22,256]{3,2,1,0:T(8,128)(2,1)S(1)}, bf16[2,3,22,256]{3,2,1,0:T(8,128)(2,1)S(1)}, u32[]{:S(2)}, u32[]{:S(2)}) collective-permute-start(bf16[2,3,22,256]{3,2,1,0:T(8,128)(2,1)S(1)} %get-tuple-element.38), channel_id=1, source_target_pairs={{8,0},{16,8},{24,16},{32,24},{40,32},{48,40},{56,48},{9,1},{17,9},... | collective-permute-start | bytes 202760 | tf_op jit(solution)/shard_map/ppermute | solution.py:415
  22.8 34.1 %copy-start = (bf16[2,22,22,256]{3,2,1,0:T(8,128)(2,1)}, bf16[2,22,22,256]{3,2,1,0:T(8,128)(2,1)S(1)}, u32[]{:S(2)}) copy-start(bf16[2,22,22,256]{3,2,1,0:T(8,128)(2,1)S(1)} %pad_maximum_fusion.wide_ref.far_wide_ref) | copy-start | bytes 1486852
  22.8 27.6 %collective-permute-start.7 = (bf16[44,22,256]{2,1,0:T(8,128)(2,1)S(1)}, bf16[44,22,256]{2,1,0:T(8,128)(2,1)S(1)}, u32[]{:S(2)}, u32[]{:S(2)}) collective-permute-start(bf16[44,22,256]{2,1,0:T(8,128)(2,1)S(1)} %bitcast.29), channel_id=1, source_target_pairs={{0,64},{64,128},{128,192},{192,0},{1,65},{65,129},{129,193},{193,1... | collective-permute-start | bytes 1486856 | tf_op jit(solution)/shard_map/ppermute | solution.py:420
  24.4 25.9 %collective-permute-start.9 = (bf16[2,10,22,256]{3,2,1,0:T(8,128)(2,1)S(1)}, bf16[2,10,22,256]{3,2,1,0:T(8,128)(2,1)S(1)}, u32[]{:S(2)}, u32[]{:S(2)}) collective-permute-start(bf16[2,10,22,256]{3,2,1,0:T(8,128)(2,1)S(1)} %get-tuple-element.33), channel_id=1, source_target_pairs={{0,192},{64,0},{128,64},{192,128},{1,193},{65,1},{129,65},{193,129... | collective-permute-start | bytes 675848 | tf_op jit(solution)/shard_map/ppermute | solution.py:420
  25.7 24.7 %collective-permute-start.8 = (bf16[2,10,22,256]{3,2,1,0:T(8,128)(2,1)S(1)}, bf16[2,10,22,256]{3,2,1,0:T(8,128)(2,1)S(1)}, u32[]{:S(2)}, u32[]{:S(2)}) collective-permute-start(bf16[2,10,22,256]{3,2,1,0:T(8,128)(2,1)S(1)} %get-tuple-element.34), channel_id=1, source_target_pairs={{0,128},{64,192},{128,0},{192,64},{1,129},{65,193},{129,1},{193,65... | collective-permute-start | bytes 675848 | tf_op jit(solution)/shard_map/ppermute | solution.py:420
  50.4 6.5 %copy-start.3 = (bf16[44,22,256]{2,1,0:T(8,128)(2,1)}, bf16[44,22,256]{2,1,0:T(8,128)(2,1)S(1)}, u32[]{:S(2)}) copy-start(bf16[44,22,256]{2,1,0:T(8,128)(2,1)S(1)} %collective-permute-done.7) | copy-start | bytes 1486852
  56.9 7.9 %collective-permute-start.12 = (f32[1,64]{1,0:T(1,128)S(1)}, f32[1,64]{1,0:T(1,128)S(1)}, u32[]{:S(2)}, u32[]{:S(2)}) collective-permute-start(f32[1,64]{1,0:T(1,128)S(1)} %slice.92), channel_id=1, source_target_pairs={{0,192},{64,0},{128,64},{192,128},{1,193},{65,1},{129,65},{193,129... | collective-permute-start | bytes 776 | tf_op jit(solution)/shard_map/ppermute | solution.py:420
  59.3 6.2 %collective-permute-start.11 = (f32[1,64]{1,0:T(1,128)S(1)}, f32[1,64]{1,0:T(1,128)S(1)}, u32[]{:S(2)}, u32[]{:S(2)}) collective-permute-start(f32[1,64]{1,0:T(1,128)S(1)} %slice.92), channel_id=1, source_target_pairs={{0,128},{64,192},{128,0},{192,64},{1,129},{65,193},{129,1},{193,65... | collective-permute-start | bytes 776 | tf_op jit(solution)/shard_map/ppermute | solution.py:420
  59.8 5.7 %collective-permute-start.10 = (f32[1,64]{1,0:T(1,128)S(1)}, f32[1,64]{1,0:T(1,128)S(1)}, u32[]{:S(2)}, u32[]{:S(2)}) collective-permute-start(f32[1,64]{1,0:T(1,128)S(1)} %slice.92), channel_id=1, source_target_pairs={{0,64},{64,128},{128,192},{192,0},{1,65},{65,129},{129,193},{193,1... | collective-permute-start | bytes 776 | tf_op jit(solution)/shard_map/ppermute | solution.py:420
  60.9 0.7 copy-start.4
  61.6 19.8 %collective-permute-start.13 = (bf16[624,256]{1,0:T(8,128)(2,1)S(1)}, bf16[624,256]{1,0:T(8,128)(2,1)S(1)}, u32[]{:S(2)}, u32[]{:S(2)}) collective-permute-start(bf16[624,256]{1,0:T(8,128)(2,1)S(1)} %get-tuple-element.30), channel_id=1, source_target_pairs={{0,64},{64,128},{128,192},{192,0},{1,65},{65,129},{129,193},{193,1... | collective-permute-start | bytes 958472 | tf_op jit(solution)/shard_map/ppermute | solution.py:420
  63.2 18.3 %collective-permute-start.14 = (bf16[624,256]{1,0:T(8,128)(2,1)S(1)}, bf16[624,256]{1,0:T(8,128)(2,1)S(1)}, u32[]{:S(2)}, u32[]{:S(2)}) collective-permute-start(bf16[624,256]{1,0:T(8,128)(2,1)S(1)} %get-tuple-element.31), channel_id=1, source_target_pairs={{0,128},{64,192},{128,0},{192,64},{1,129},{65,193},{129,1},{193,65... | collective-permute-start | bytes 958472 | tf_op jit(solution)/shard_map/ppermute | solution.py:420
  64.9 16.6 %collective-permute-start.15 = (bf16[624,256]{1,0:T(8,128)(2,1)S(1)}, bf16[624,256]{1,0:T(8,128)(2,1)S(1)}, u32[]{:S(2)}, u32[]{:S(2)}) collective-permute-start(bf16[624,256]{1,0:T(8,128)(2,1)S(1)} %get-tuple-element.32), channel_id=1, source_target_pairs={{0,192},{64,0},{128,64},{192,128},{1,193},{65,1},{129,65},{193,129... | collective-permute-start | bytes 958472 | tf_op jit(solution)/shard_map/ppermute | solution.py:420
  81.5 0.7 copy-start.8
  81.5 0.8 copy-start.9
  81.5 1.0 copy-start.10
